TPU v7x, 512 devices: a whole 4x4x16 slice. The times are simulated.
512 devices in a mesh: mem: 16 (over x, z_lo), lat: 4 (over z_hi), win: 8 (over y, core).
Axes of the slice: x: 4, y: 4, z: 16 (z_hi: 4, z_lo: 4; z = z_hi * 4 + z_lo), core: 2. Of those that a mesh axis runs over, the one named last changes fastest.
Arguments:
- ensemble: float32 [32, 8, 32, 2048], P('mem', None, 'lat'), may hold values from -6 to 6
- weights: float32 [8, 32, 32, 2048], P('win', 'mem', 'lat'), may hold values from -6 to 6
- diffusivity: float32 [8, 32, 2048], P(None, 'lat', 'mem'), may hold values from 0.05 to 0.4
- coupling: float32 [8, 8], replicated, may hold values from -0.5 to 0.5
- tl_steps: int32 [8], P('win'), may hold values from 1 to 6
- obs_cell: int32 [65536], P(('mem', 'lat')), may hold values from 0 to 8191
- obs_window: int32 [65536], P(('mem', 'lat')), may hold values from 0 to 7
- obs_value: float32 [65536], P(('mem', 'lat')), may hold values from -6 to 6
- obs_weight: float32 [65536], P(('mem', 'lat')), may hold values from 1 to 8
- error_weight: float32 [8], replicated, may hold values from 0.5 to 4
Outputs:
- control: float32 [8, 32, 32, 2048], P('win', 'mem', 'lat')
- increment: float32 [8, 8, 32, 2048], P('win', None, 'lat', 'mem')
Inputs may be any that keep to these rules, and one draw needn't show every extreme that they name: `tl_steps`: how many of the 6 tangent steps the subwindow takes. `obs_cell`: index of the observed cell in the block of 8 x 8 x 128 cells that the observation's device holds (mem index, lat index), flattened as variable, row, longitude.
All inputs are finite; a program needn't handle non-finite values.
Results may differ from a plain program's by a relative error of at most 0.00015.
Values sent between devices are 32-bit elements; how exact they have to be, the bound alone decides.
A program may use at most 64 MiB of HBM per device.

v0:
```python
import math

import jax
import jax.numpy as jnp
from jax import lax
from jax.sharding import PartitionSpec as P

KMAX = 6
DIFF = 2
ITERS = 2


KAPPA = 0.125
DESCENT = 0.25
HIGHEST = lax.Precision.HIGHEST


def with_halo(x, sides, width):
    for axis, dim in sides:
        peers, length = (lax.axis_size(axis), x.shape[dim])
        up = [(i, (i + 1) % peers) for i in range(peers - 1)]
        down = [(j, i) for i, j in up]
        last = lax.slice_in_dim(x, length - width, length, axis=dim)
        initial = lax.slice_in_dim(x, 0, width, axis=dim)
        before = lax.ppermute(last, axis, up)
        after = lax.ppermute(initial, axis, down)
        x = jnp.concatenate([before, x, after], axis=dim)
    return x


def split_up(x, dim, peers):
    lengths = x.shape
    parts = x.reshape(*lengths[:dim], peers, lengths[dim] // peers, *lengths[dim + 1 :])
    return jnp.moveaxis(parts, dim, 0)


def sum_at_owner(x, axis, dim):
    parts = split_up(x, dim, lax.axis_size(axis))
    arrived = lax.all_to_all(parts, axis, split_axis=0, concat_axis=0, tiled=True)
    return arrived.sum(axis=0)


def from_behind(block, axis, distance):
    devices = range(lax.axis_size(axis))
    route = [(i - distance, i) for i in devices if i - distance in devices]
    return lax.ppermute(block, axis, route)


def copy_for_each(x, axis):
    peers = lax.axis_size(axis)
    return lax.all_to_all(jnp.broadcast_to(x[None], (peers, *x.shape)), axis, 0, 0, tiled=True)


def laid_out(parts, dim):
    lengths = list(parts.shape[1:])
    lengths[dim] *= parts.shape[0]
    return jnp.moveaxis(parts, 0, dim).reshape(lengths)


def gathered_copies(x, axis, dim):
    parts = copy_for_each(x, axis)
    return laid_out(parts, dim)


def relax(padded):
    middle = padded[:, 1:-1, :]
    beside_all = (
        padded[:, 2:, :] + padded[:, :-2, :] + jnp.roll(middle, 1, -1) + jnp.roll(middle, -1, -1)
    )
    return middle + KAPPA * (beside_all - 4.0 * middle)


def inside_mask(rows, width):
    anchor = lax.axis_index("lat") * rows - width
    global_rows = anchor + jnp.arange(rows + 2 * width, dtype=jnp.int32)
    return (global_rows >= 0) & (global_rows < rows * lax.axis_size("lat"))


def smooth(values):
    rows = values.shape[1]
    padded = with_halo(values, (("lat", 1),), DIFF)
    inside_rows = inside_mask(rows, DIFF)
    for repeat in range(DIFF):
        padded = relax(padded)
        keep = inside_rows[repeat + 1 : rows + 2 * DIFF - repeat - 1]
        padded = jnp.where(keep[None, :, None], padded, 0.0)
    return padded


def forward(state, wide_coeff, coupling, step_count):
    rows = state.shape[1]
    total = rows + 2 * KMAX
    inside_rows = inside_mask(rows, KMAX)
    current = with_halo(state, (("lat", 1),), KMAX)
    for section_index in range(KMAX):
        center = current[:, 1:-1]
        second = current[:, 2:] + current[:, :-2] - 2.0 * center
        coeff = wide_coeff[:, section_index + 1 : total - section_index - 1]
        mixed = jnp.einsum("vu,url->vrl", coupling, center, precision=HIGHEST)
        moved = center + coeff * second + mixed
        keep = inside_rows[section_index + 1 : total - section_index - 1]
        moved = jnp.where(keep[None, :, None], moved, 0.0)
        current = jnp.where(section_index < step_count, moved, center)
    state = current
    return state


def backward(state, wide_coeff, coupling, step_count):
    rows = state.shape[1]
    total = rows + 2 * KMAX
    inside_rows = inside_mask(rows, KMAX)
    current = with_halo(state, (("lat", 1),), KMAX)
    for depth_index in range(KMAX):
        section_index = KMAX - 1 - depth_index
        coeff = wide_coeff[:, depth_index : total - depth_index]
        weighted = coeff * current
        center = current[:, 1:-1]
        second = weighted[:, 2:] + weighted[:, :-2] - 2.0 * weighted[:, 1:-1]
        mixed = jnp.einsum("uv,url->vrl", coupling, center, precision=HIGHEST)
        moved = center + second + mixed
        keep = inside_rows[depth_index + 1 : total - depth_index - 1]
        moved = jnp.where(keep[None, :, None], moved, 0.0)
        current = jnp.where(section_index < step_count, moved, center)
    state = current
    return state


def local(
    ensemble,
    weights,
    diffusivity,
    coupling,
    tl_steps,
    obs_cell,
    obs_window,
    obs_value,
    obs_weight,
    error_weight,
):
    members = ensemble.shape[0] * lax.axis_size("mem")
    member_scale = 1.0 / math.sqrt(members - 1)
    control = weights[0]
    step_count = tl_steps[0]
    window = lax.axis_index("win")
    has_before = window > 0
    wide_coeff = None
    wide_coeff = with_halo(diffusivity, (("lat", 1),), KMAX)
    increment = None
    for iteration in range(ITERS):
        smoothed = smooth(control)
        partial_sum = (
            jnp.einsum("mvrl,mrl->vrl", ensemble, smoothed, precision=HIGHEST) * member_scale
        )
        increment = sum_at_owner(partial_sum, "mem", 2)
        ends = forward(increment, wide_coeff, coupling, step_count)
        previous = from_behind(ends, "win", 1)
        misfit = jnp.where(has_before, error_weight[:, None, None] * (previous - increment), 0.0)
        misfit_next = from_behind(misfit, "win", -1)
        flat_state = ends.reshape(-1)
        picked = flat_state[obs_cell]
        innovation = jnp.where(obs_window == window, (picked - obs_value) * obs_weight, 0.0)
        observed = jnp.zeros_like(flat_state).at[obs_cell].add(innovation).reshape(ends.shape)
        gradient = backward(observed + misfit_next, wide_coeff, coupling, step_count) - misfit
        whole_gradient = gathered_copies(gradient, "mem", 2)
        back_members = (
            jnp.einsum("mvrl,vrl->mrl", ensemble, whole_gradient, precision=HIGHEST) * member_scale
        )
        control = control - DESCENT * (control + smooth(back_members))
    return (control[None], increment[None])


def solution(mesh):
    return jax.shard_map(
        local,
        mesh=mesh,
        in_specs=(
            P("mem", None, "lat", None),
            P("win", "mem", "lat", None),
            P(None, "lat", "mem"),
            P(),
            P("win"),
            P(("mem", "lat")),
            P(("mem", "lat")),
            P(("mem", "lat")),
            P(("mem", "lat")),
            P(),
        ),
        out_specs=(P("win", "mem", "lat", None), P("win", None, "lat", "mem")),
        check_vma=False,
    )
```

profile of v0, /device:TPU:24, one launch (start us, length us, event | category | flops | bytes accessed | tf_op | source)
XLA Modules:
  0.0 238.0 jit_solution(9276381842663121189)
XLA Ops:
  0.7 1.1 fusion.268
  1.7 9.1 %collective-permute-start = (f32[2,2,2048]{2,1,0:T(2,128)S(1)}, f32[2,2,2048]{2,1,0:T(2,128)S(1)}, u32[]{:S(2)}, u32[]{:S(2)}) collective-permute-start(f32[2,2,2048]{2,1,0:T(2,128)S(1)} %get-tuple-element.42), channel_id=1, source_target_pairs={{0,8},{8,16},{16,24},{1,9},{9,17},{17,25},{2,10},{10,18},{18,26},{... | collective-permute-start | bytes 98312 | tf_op jit(solution)/shard_map/ppermute | solution.py:25
  10.8 1.3 collective-permute-start.1
  12.4 10.1 %collective-permute-done.1 = f32[2,2,2048]{2,1,0:T(2,128)S(1)} collective-permute-done((f32[2,2,2048]{2,1,0:T(2,128)S(1)}, f32[2,2,2048]{2,1,0:T(2,128)S(1)}, u32[]{:S(2)}, u32[]{:S(2)}) %collective-permute-start.1) | collective-permute-done | bytes 32800 | tf_op jit(solution)/shard_map/ppermute | solution.py:26
  23.2 0.7 copy-done.1
  24.2 1.0 copy.110
  25.2 6.6 %all-to-all-start = ((f32[16,8,8,128]{3,2,1,0:T(8,128)}), f32[16,8,8,128]{3,2,1,0:T(8,128)S(1)}, u32[]{:S(2)}, u32[]{:S(2)}) async-start(f32[16,8,8,128]{3,2,1,0:T(8,128)} %copy.110), calls=%async_computation | async-start | bytes 1048576 | tf_op jit(solution)/shard_map/all_to_all | solution.py:39
  31.8 6.7 %collective-permute-start.4 = (f32[8,6,128]{2,0,1:T(8,128)S(1)}, f32[8,6,128]{2,0,1:T(8,128)S(1)}, u32[]{:S(2)}, u32[]{:S(2)}) collective-permute-start(f32[8,6,128]{2,0,1:T(8,128)S(1)} %copy.222), channel_id=1, source_target_pairs={{0,8},{8,16},{16,24},{1,9},{9,17},{17,25},{2,10},{10,18},{18,26},{... | collective-permute-start | bytes 73736 | tf_op jit(solution)/shard_map/ppermute | solution.py:25
  38.6 1.3 collective-permute-start.5
  41.1 5.9 %all-to-all-done = f32[16,8,8,128]{3,2,1,0:T(8,128)S(1)} async-done(((f32[16,8,8,128]{3,2,1,0:T(8,128)}), f32[16,8,8,128]{3,2,1,0:T(8,128)S(1)}, u32[]{:S(2)}, u32[]{:S(2)}) %all-to-all-start) | async-done | bytes 524320 | tf_op jit(solution)/shard_map/all_to_all | solution.py:39
  47.0 7.5 %collective-permute-start.2 = (f32[8,6,128]{2,0,1:T(8,128)S(1)}, f32[8,6,128]{2,0,1:T(8,128)S(1)}, u32[]{:S(2)}, u32[]{:S(2)}) collective-permute-start(f32[8,6,128]{2,0,1:T(8,128)S(1)} %copy.220), channel_id=1, source_target_pairs={{0,8},{8,16},{16,24},{1,9},{9,17},{17,25},{2,10},{10,18},{18,26},{... | collective-permute-start | bytes 73736 | tf_op jit(solution)/shard_map/ppermute | solution.py:25
  54.6 1.3 collective-permute-start.3
  56.0 8.2 %collective-permute-done.3 = f32[8,6,128]{2,0,1:T(8,128)S(1)} collective-permute-done((f32[8,6,128]{2,0,1:T(8,128)S(1)}, f32[8,6,128]{2,0,1:T(8,128)S(1)}, u32[]{:S(2)}, u32[]{:S(2)}) %collective-permute-start.3) | collective-permute-done | bytes 24608 | tf_op jit(solution)/shard_map/ppermute | solution.py:26
  65.4 1.9 collective-permute-start.6
  67.3 6.2 %gather_fusion = f32[1024]{0:T(1024)S(1)} fusion(f32[8192]{0:T(1024)S(1)} %bitcast.351, s32[1024]{0:T(1024)S(1)} %get-tuple-element.58), kind=kCustom, calls=%fused_computation | custom fusion | bytes 12288 | tf_op jit(solution)/shard_map/gather | solution.py:160
  73.6 3.6 %collective-permute-start.7 = (f32[8,8,128]{2,0,1:T(8,128)S(1)}, f32[8,8,128]{2,0,1:T(8,128)S(1)}, u32[]{:S(2)}, u32[]{:S(2)}) collective-permute-start(f32[8,8,128]{2,0,1:T(8,128)S(1)} %multiply_select_fusion.1), channel_id=1, source_target_pairs={{1,0},{2,1},{3,2},{4,3},{5,4},{6,5},{7,6},{9,8},{10,9},{11,10},{12... | collective-permute-start | bytes 98312 | tf_op jit(solution)/shard_map/ppermute | solution.py:46
  77.3 5.9 %scatter_custom_fusion = f32[8192]{0:T(1024)S(1)} fusion(s32[1024]{0:T(1024)S(1)} %get-tuple-element.59, f32[1024]{0:T(1024)S(1)} %get-tuple-element.10, f32[]{:T(128)} %constant.11.clone.1), kind=kCustom, calls=%fused_computation.332 | custom fusion | flops 1024 | bytes 32772 | tf_op jit(solution)/shard_map/scatter-add | solution.py:162
  83.3 5.2 %collective-permute-start.8 = (f32[8,6,128]{2,0,1:T(8,128)S(1)}, f32[8,6,128]{2,0,1:T(8,128)S(1)}, u32[]{:S(2)}, u32[]{:S(2)}) collective-permute-start(f32[8,6,128]{2,0,1:T(8,128)S(1)} %get-tuple-element.52), channel_id=1, source_target_pairs={{0,8},{8,16},{16,24},{1,9},{9,17},{17,25},{2,10},{10,18},{18,26},{... | collective-permute-start | bytes 73736 | tf_op jit(solution)/shard_map/ppermute | solution.py:25
  88.6 1.3 collective-permute-start.9
  90.1 8.3 %collective-permute-done.9 = f32[8,6,128]{2,0,1:T(8,128)S(1)} collective-permute-done((f32[8,6,128]{2,0,1:T(8,128)S(1)}, f32[8,6,128]{2,0,1:T(8,128)S(1)}, u32[]{:S(2)}, u32[]{:S(2)}) %collective-permute-start.9) | collective-permute-done | bytes 24608 | tf_op jit(solution)/shard_map/ppermute | solution.py:26
  98.4 0.3 slice_multiply_fusion.5
  100.0 18.3 %all_to_all.20 = f32[16,8,8,128]{3,2,1,0:T(8,128)S(1)} all-to-all(f32[16,8,8,128]{3,2,1,0:T(8,128)S(1)} %broadcast_in_dim.276), channel_id=1, replica_groups=mesh['mem'=16,'lat'=4,'win'=8] {'mem'}, dimensions={0} | all-to-all | bytes 1048576 | tf_op jit(solution)/shard_map/all_to_all | solution.py:51
  118.5 4.0 %collective-permute-start.10 = (f32[2,2,2048]{2,1,0:T(2,128)S(1)}, f32[2,2,2048]{2,1,0:T(2,128)S(1)}, u32[]{:S(2)}, u32[]{:S(2)}) collective-permute-start(f32[2,2,2048]{2,1,0:T(2,128)S(1)} %get-tuple-element.40), channel_id=1, source_target_pairs={{0,8},{8,16},{16,24},{1,9},{9,17},{17,25},{2,10},{10,18},{18,26},{... | collective-permute-start | bytes 98312 | tf_op jit(solution)/shard_map/ppermute | solution.py:25
  122.5 1.3 collective-permute-start.11
  123.8 0.3 collective-permute-done.10
  124.1 8.1 %collective-permute-done.11 = f32[2,2,2048]{2,1,0:T(2,128)S(1)} collective-permute-done((f32[2,2,2048]{2,1,0:T(2,128)S(1)}, f32[2,2,2048]{2,1,0:T(2,128)S(1)}, u32[]{:S(2)}, u32[]{:S(2)}) %collective-permute-start.11) | collective-permute-done | bytes 32800 | tf_op jit(solution)/shard_map/ppermute | solution.py:26
  133.0 2.6 %collective-permute-start.12 = (f32[2,2,2048]{2,1,0:T(2,128)S(1)}, f32[2,2,2048]{2,1,0:T(2,128)S(1)}, u32[]{:S(2)}, u32[]{:S(2)}) collective-permute-start(f32[2,2,2048]{2,1,0:T(2,128)S(1)} %get-tuple-element.38), channel_id=1, source_target_pairs={{0,8},{8,16},{16,24},{1,9},{9,17},{17,25},{2,10},{10,18},{18,26},{... | collective-permute-start | bytes 98312 | tf_op jit(solution)/shard_map/ppermute | solution.py:25
  135.6 1.3 collective-permute-start.13
  136.9 0.3 collective-permute-done.12
  137.2 8.4 %collective-permute-done.13 = f32[2,2,2048]{2,1,0:T(2,128)S(1)} collective-permute-done((f32[2,2,2048]{2,1,0:T(2,128)S(1)}, f32[2,2,2048]{2,1,0:T(2,128)S(1)}, u32[]{:S(2)}, u32[]{:S(2)}) %collective-permute-start.13) | collective-permute-done | bytes 32800 | tf_op jit(solution)/shard_map/ppermute | solution.py:26
  146.7 15.5 %all_to_all.21 = f32[16,8,8,128]{3,2,1,0:T(8,128)S(1)} all-to-all(f32[16,8,8,128]{3,2,1,0:T(8,128)S(1)} %copy.129), channel_id=1, replica_groups=mesh['mem'=16,'lat'=4,'win'=8] {'mem'}, dimensions={0} | all-to-all | bytes 1048576 | tf_op jit(solution)/shard_map/all_to_all | solution.py:39
  162.3 1.9 collective-permute-start.14
  164.2 1.3 collective-permute-start.15
  165.7 8.1 %collective-permute-done.15 = f32[8,6,128]{2,0,1:T(8,128)S(1)} collective-permute-done((f32[8,6,128]{2,0,1:T(8,128)S(1)}, f32[8,6,128]{2,0,1:T(8,128)S(1)}, u32[]{:S(2)}, u32[]{:S(2)}) %collective-permute-start.15) | collective-permute-done | bytes 24608 | tf_op jit(solution)/shard_map/ppermute | solution.py:26
  175.0 1.9 collective-permute-start.16
  176.9 6.2 %gather_fusion.1 = f32[1024]{0:T(1024)S(1)} fusion(f32[8192]{0:T(1024)S(1)} %bitcast.350, s32[1024]{0:T(1024)S(1)} %get-tuple-element.58), kind=kCustom, calls=%fused_computation.1 | custom fusion | bytes 12288 | tf_op jit(solution)/shard_map/gather | solution.py:160
  183.2 3.6 %collective-permute-start.17 = (f32[8,8,128]{2,0,1:T(8,128)S(1)}, f32[8,8,128]{2,0,1:T(8,128)S(1)}, u32[]{:S(2)}, u32[]{:S(2)}) collective-permute-start(f32[8,8,128]{2,0,1:T(8,128)S(1)} %multiply_select_fusion), channel_id=1, source_target_pairs={{1,0},{2,1},{3,2},{4,3},{5,4},{6,5},{7,6},{9,8},{10,9},{11,10},{12... | collective-permute-start | bytes 98312 | tf_op jit(solution)/shard_map/ppermute | solution.py:46
  186.9 5.9 %scatter_custom_fusion.1 = f32[8192]{0:T(1024)S(1)} fusion(s32[1024]{0:T(1024)S(1)} %get-tuple-element.59, f32[1024]{0:T(1024)S(1)} %multiply_select_fusion.2, f32[]{:T(128)} %constant.11.clone.1), kind=kCustom, calls=%fused_computation.330 | custom fusion | flops 1024 | bytes 32772 | tf_op jit(solution)/shard_map/scatter-add | solution.py:162
  192.9 1.9 collective-permute-start.18
  194.8 1.3 collective-permute-start.19
  196.3 8.1 %collective-permute-done.19 = f32[8,6,128]{2,0,1:T(8,128)S(1)} collective-permute-done((f32[8,6,128]{2,0,1:T(8,128)S(1)}, f32[8,6,128]{2,0,1:T(8,128)S(1)}, u32[]{:S(2)}, u32[]{:S(2)}) %collective-permute-start.19) | collective-permute-done | bytes 24608 | tf_op jit(solution)/shard_map/ppermute | solution.py:26
  204.4 0.3 slice_multiply_fusion.4
  206.0 17.5 %all_to_all.22 = f32[16,8,8,128]{3,2,1,0:T(8,128)S(1)} all-to-all(f32[16,8,8,128]{3,2,1,0:T(8,128)S(1)} %broadcast_in_dim.277), channel_id=1, replica_groups=mesh['mem'=16,'lat'=4,'win'=8] {'mem'}, dimensions={0} | all-to-all | bytes 1048576 | tf_op jit(solution)/shard_map/all_to_all | solution.py:51
  223.7 2.9 %collective-permute-start.20 = (f32[2,2,2048]{2,1,0:T(2,128)S(1)}, f32[2,2,2048]{2,1,0:T(2,128)S(1)}, u32[]{:S(2)}, u32[]{:S(2)}) collective-permute-start(f32[2,2,2048]{2,1,0:T(2,128)S(1)} %get-tuple-element.36), channel_id=1, source_target_pairs={{0,8},{8,16},{16,24},{1,9},{9,17},{17,25},{2,10},{10,18},{18,26},{... | collective-permute-start | bytes 98312 | tf_op jit(solution)/shard_map/ppermute | solution.py:25
  226.7 1.3 collective-permute-start.21
  228.0 0.3 collective-permute-done.20
  228.2 8.5 %collective-permute-done.21 = f32[2,2,2048]{2,1,0:T(2,128)S(1)} collective-permute-done((f32[2,2,2048]{2,1,0:T(2,128)S(1)}, f32[2,2,2048]{2,1,0:T(2,128)S(1)}, u32[]{:S(2)}, u32[]{:S(2)}) %collective-permute-start.21) | collective-permute-done | bytes 32800 | tf_op jit(solution)/shard_map/ppermute | solution.py:26
  237.2 0.8 fusion.79
  (138 shorter events, 10.3 us)
Async XLA Ops:
  0.6 63.6 %copy-start = (f32[8,8]{1,0:T(8,128)S(1)}, f32[8,8]{1,0:T(8,128)}, u32[]{:S(2)}) copy-start(f32[8,8]{1,0:T(8,128)} %param.13) | copy-start | bytes 772
  0.6 21.9 %copy-start.2 = (f32[1,2,8,2048]{3,2,1,0:T(8,128)S(1)}, f32[1,2,8,2048]{3,2,1,0:T(8,128)}, u32[]{:S(2)}) copy-start(f32[1,2,8,2048]{3,2,1,0:T(8,128)} %param.11) | copy-start | bytes 393220
  1.7 10.7 %collective-permute-start = (f32[2,2,2048]{2,1,0:T(2,128)S(1)}, f32[2,2,2048]{2,1,0:T(2,128)S(1)}, u32[]{:S(2)}, u32[]{:S(2)}) collective-permute-start(f32[2,2,2048]{2,1,0:T(2,128)S(1)} %get-tuple-element.42), channel_id=1, source_target_pairs={{0,8},{8,16},{16,24},{1,9},{9,17},{17,25},{2,10},{10,18},{18,26},{... | collective-permute-start | bytes 98312 | tf_op jit(solution)/shard_map/ppermute | solution.py:25
  10.8 11.7 %collective-permute-start.1 = (f32[2,2,2048]{2,1,0:T(2,128)S(1)}, f32[2,2,2048]{2,1,0:T(2,128)S(1)}, u32[]{:S(2)}, u32[]{:S(2)}) collective-permute-start(f32[2,2,2048]{2,1,0:T(2,128)S(1)} %get-tuple-element.43), channel_id=1, source_target_pairs={{8,0},{16,8},{24,16},{9,1},{17,9},{25,17},{10,2},{18,10},{26,18},{... | collective-permute-start | bytes 98312 | tf_op jit(solution)/shard_map/ppermute | solution.py:26
  22.7 1.2 copy-start.1
  25.2 6.6 %copy-start.4 = (f32[8,8,128]{2,1,0:T(8,128)S(1)}, f32[8,8,128]{2,1,0:T(8,128)}, u32[]{:S(2)}) copy-start(f32[8,8,128]{2,1,0:T(8,128)} %param.12) | copy-start | bytes 98308
  25.2 21.7 %all-to-all-start = ((f32[16,8,8,128]{3,2,1,0:T(8,128)}), f32[16,8,8,128]{3,2,1,0:T(8,128)S(1)}, u32[]{:S(2)}, u32[]{:S(2)}) async-start(f32[16,8,8,128]{3,2,1,0:T(8,128)} %copy.110), calls=%async_computation | async-start | bytes 1048576 | tf_op jit(solution)/shard_map/all_to_all | solution.py:39
  31.8 9.2 %collective-permute-start.4 = (f32[8,6,128]{2,0,1:T(8,128)S(1)}, f32[8,6,128]{2,0,1:T(8,128)S(1)}, u32[]{:S(2)}, u32[]{:S(2)}) collective-permute-start(f32[8,6,128]{2,0,1:T(8,128)S(1)} %copy.222), channel_id=1, source_target_pairs={{0,8},{8,16},{16,24},{1,9},{9,17},{17,25},{2,10},{10,18},{18,26},{... | collective-permute-start | bytes 73736 | tf_op jit(solution)/shard_map/ppermute | solution.py:25
  38.6 16.0 %collective-permute-start.5 = (f32[8,6,128]{2,0,1:T(8,128)S(1)}, f32[8,6,128]{2,0,1:T(8,128)S(1)}, u32[]{:S(2)}, u32[]{:S(2)}) collective-permute-start(f32[8,6,128]{2,0,1:T(8,128)S(1)} %copy.223), channel_id=1, source_target_pairs={{8,0},{16,8},{24,16},{9,1},{17,9},{25,17},{10,2},{18,10},{26,18},{... | collective-permute-start | bytes 73736 | tf_op jit(solution)/shard_map/ppermute | solution.py:26
  47.0 9.1 %collective-permute-start.2 = (f32[8,6,128]{2,0,1:T(8,128)S(1)}, f32[8,6,128]{2,0,1:T(8,128)S(1)}, u32[]{:S(2)}, u32[]{:S(2)}) collective-permute-start(f32[8,6,128]{2,0,1:T(8,128)S(1)} %copy.220), channel_id=1, source_target_pairs={{0,8},{8,16},{16,24},{1,9},{9,17},{17,25},{2,10},{10,18},{18,26},{... | collective-permute-start | bytes 73736 | tf_op jit(solution)/shard_map/ppermute | solution.py:25
  54.6 9.6 %collective-permute-start.3 = (f32[8,6,128]{2,0,1:T(8,128)S(1)}, f32[8,6,128]{2,0,1:T(8,128)S(1)}, u32[]{:S(2)}, u32[]{:S(2)}) collective-permute-start(f32[8,6,128]{2,0,1:T(8,128)S(1)} %copy.221), channel_id=1, source_target_pairs={{8,0},{16,8},{24,16},{9,1},{17,9},{25,17},{10,2},{18,10},{26,18},{... | collective-permute-start | bytes 73736 | tf_op jit(solution)/shard_map/ppermute | solution.py:26
  65.2 2.1 copy-start.7
  65.4 8.2 %collective-permute-start.6 = (f32[8,8,128]{2,0,1:T(8,128)S(1)}, f32[8,8,128]{2,0,1:T(8,128)S(1)}, u32[]{:S(2)}, u32[]{:S(2)}) collective-permute-start(f32[8,8,128]{2,0,1:T(8,128)S(1)} %fusion.37), channel_id=1, source_target_pairs={{0,1},{1,2},{2,3},{3,4},{4,5},{5,6},{6,7},{8,9},{9,10},{10,11},{11... | collective-permute-start | bytes 98312 | tf_op jit(solution)/shard_map/ppermute | solution.py:46
  67.3 6.2 %copy-start.9 = (f32[8]{0:T(128)S(1)}, f32[8]{0:T(128)}, u32[]{:S(2)}) copy-start(f32[8]{0:T(128)} %param.19) | copy-start | bytes 100
  73.5 3.8 %copy-start.5 = (f32[1024]{0:T(1024)S(1)}, f32[1024]{0:T(1024)}, u32[]{:S(2)}) copy-start(f32[1024]{0:T(1024)} %param.18) | copy-start | bytes 12292
  73.5 3.8 %copy-start.6 = (f32[1024]{0:T(1024)S(1)}, f32[1024]{0:T(1024)}, u32[]{:S(2)}) copy-start(f32[1024]{0:T(1024)} %param.17) | copy-start | bytes 12292
  73.5 3.8 %copy-start.8 = (s32[1024]{0:T(1024)S(1)}, s32[1024]{0:T(1024)}, u32[]{:S(2)}) copy-start(s32[1024]{0:T(1024)} %param.16) | copy-start | bytes 12292
  73.6 9.6 %collective-permute-start.7 = (f32[8,8,128]{2,0,1:T(8,128)S(1)}, f32[8,8,128]{2,0,1:T(8,128)S(1)}, u32[]{:S(2)}, u32[]{:S(2)}) collective-permute-start(f32[8,8,128]{2,0,1:T(8,128)S(1)} %multiply_select_fusion.1), channel_id=1, source_target_pairs={{1,0},{2,1},{3,2},{4,3},{5,4},{6,5},{7,6},{9,8},{10,9},{11,10},{12... | collective-permute-start | bytes 98312 | tf_op jit(solution)/shard_map/ppermute | solution.py:46
  83.3 6.7 %collective-permute-start.8 = (f32[8,6,128]{2,0,1:T(8,128)S(1)}, f32[8,6,128]{2,0,1:T(8,128)S(1)}, u32[]{:S(2)}, u32[]{:S(2)}) collective-permute-start(f32[8,6,128]{2,0,1:T(8,128)S(1)} %get-tuple-element.52), channel_id=1, source_target_pairs={{0,8},{8,16},{16,24},{1,9},{9,17},{17,25},{2,10},{10,18},{18,26},{... | collective-permute-start | bytes 73736 | tf_op jit(solution)/shard_map/ppermute | solution.py:25
  88.6 9.8 %collective-permute-start.9 = (f32[8,6,128]{2,0,1:T(8,128)S(1)}, f32[8,6,128]{2,0,1:T(8,128)S(1)}, u32[]{:S(2)}, u32[]{:S(2)}) collective-permute-start(f32[8,6,128]{2,0,1:T(8,128)S(1)} %get-tuple-element.53), channel_id=1, source_target_pairs={{8,0},{16,8},{24,16},{9,1},{17,9},{25,17},{10,2},{18,10},{26,18},{... | collective-permute-start | bytes 73736 | tf_op jit(solution)/shard_map/ppermute | solution.py:26
  118.5 5.6 %collective-permute-start.10 = (f32[2,2,2048]{2,1,0:T(2,128)S(1)}, f32[2,2,2048]{2,1,0:T(2,128)S(1)}, u32[]{:S(2)}, u32[]{:S(2)}) collective-permute-start(f32[2,2,2048]{2,1,0:T(2,128)S(1)} %get-tuple-element.40), channel_id=1, source_target_pairs={{0,8},{8,16},{16,24},{1,9},{9,17},{17,25},{2,10},{10,18},{18,26},{... | collective-permute-start | bytes 98312 | tf_op jit(solution)/shard_map/ppermute | solution.py:25
  122.5 9.7 %collective-permute-start.11 = (f32[2,2,2048]{2,1,0:T(2,128)S(1)}, f32[2,2,2048]{2,1,0:T(2,128)S(1)}, u32[]{:S(2)}, u32[]{:S(2)}) collective-permute-start(f32[2,2,2048]{2,1,0:T(2,128)S(1)} %get-tuple-element.41), channel_id=1, source_target_pairs={{8,0},{16,8},{24,16},{9,1},{17,9},{25,17},{10,2},{18,10},{26,18},{... | collective-permute-start | bytes 98312 | tf_op jit(solution)/shard_map/ppermute | solution.py:26
  133.0 4.2 %collective-permute-start.12 = (f32[2,2,2048]{2,1,0:T(2,128)S(1)}, f32[2,2,2048]{2,1,0:T(2,128)S(1)}, u32[]{:S(2)}, u32[]{:S(2)}) collective-permute-start(f32[2,2,2048]{2,1,0:T(2,128)S(1)} %get-tuple-element.38), channel_id=1, source_target_pairs={{0,8},{8,16},{16,24},{1,9},{9,17},{17,25},{2,10},{10,18},{18,26},{... | collective-permute-start | bytes 98312 | tf_op jit(solution)/shard_map/ppermute | solution.py:25
  135.6 9.9 %collective-permute-start.13 = (f32[2,2,2048]{2,1,0:T(2,128)S(1)}, f32[2,2,2048]{2,1,0:T(2,128)S(1)}, u32[]{:S(2)}, u32[]{:S(2)}) collective-permute-start(f32[2,2,2048]{2,1,0:T(2,128)S(1)} %get-tuple-element.39), channel_id=1, source_target_pairs={{8,0},{16,8},{24,16},{9,1},{17,9},{25,17},{10,2},{18,10},{26,18},{... | collective-permute-start | bytes 98312 | tf_op jit(solution)/shard_map/ppermute | solution.py:26
  162.2 20.9 %copy-start.3 = (f32[8,8,128]{2,1,0:T(8,128)}, f32[8,8,128]{2,1,0:T(8,128)S(1)}, u32[]{:S(2)}) copy-start(f32[8,8,128]{2,1,0:T(8,128)S(1)} %reduce_sum.19) | copy-start | bytes 98308
  162.3 3.4 %collective-permute-start.14 = (f32[8,6,128]{2,0,1:T(8,128)S(1)}, f32[8,6,128]{2,0,1:T(8,128)S(1)}, u32[]{:S(2)}, u32[]{:S(2)}) collective-permute-start(f32[8,6,128]{2,0,1:T(8,128)S(1)} %copy.224), channel_id=1, source_target_pairs={{0,8},{8,16},{16,24},{1,9},{9,17},{17,25},{2,10},{10,18},{18,26},{... | collective-permute-start | bytes 73736 | tf_op jit(solution)/shard_map/ppermute | solution.py:25
  164.2 9.6 %collective-permute-start.15 = (f32[8,6,128]{2,0,1:T(8,128)S(1)}, f32[8,6,128]{2,0,1:T(8,128)S(1)}, u32[]{:S(2)}, u32[]{:S(2)}) collective-permute-start(f32[8,6,128]{2,0,1:T(8,128)S(1)} %copy.225), channel_id=1, source_target_pairs={{8,0},{16,8},{24,16},{9,1},{17,9},{25,17},{10,2},{18,10},{26,18},{... | collective-permute-start | bytes 73736 | tf_op jit(solution)/shard_map/ppermute | solution.py:26
  175.0 8.1 %collective-permute-start.16 = (f32[8,8,128]{2,0,1:T(8,128)S(1)}, f32[8,8,128]{2,0,1:T(8,128)S(1)}, u32[]{:S(2)}, u32[]{:S(2)}) collective-permute-start(f32[8,8,128]{2,0,1:T(8,128)S(1)} %fusion.30), channel_id=1, source_target_pairs={{0,1},{1,2},{2,3},{3,4},{4,5},{5,6},{6,7},{8,9},{9,10},{10,11},{11... | collective-permute-start | bytes 98312 | tf_op jit(solution)/shard_map/ppermute | solution.py:46
  183.2 9.6 %collective-permute-start.17 = (f32[8,8,128]{2,0,1:T(8,128)S(1)}, f32[8,8,128]{2,0,1:T(8,128)S(1)}, u32[]{:S(2)}, u32[]{:S(2)}) collective-permute-start(f32[8,8,128]{2,0,1:T(8,128)S(1)} %multiply_select_fusion), channel_id=1, source_target_pairs={{1,0},{2,1},{3,2},{4,3},{5,4},{6,5},{7,6},{9,8},{10,9},{11,10},{12... | collective-permute-start | bytes 98312 | tf_op jit(solution)/shard_map/ppermute | solution.py:46
  192.9 3.4 %collective-permute-start.18 = (f32[8,6,128]{2,0,1:T(8,128)S(1)}, f32[8,6,128]{2,0,1:T(8,128)S(1)}, u32[]{:S(2)}, u32[]{:S(2)}) collective-permute-start(f32[8,6,128]{2,0,1:T(8,128)S(1)} %get-tuple-element.48), channel_id=1, source_target_pairs={{0,8},{8,16},{16,24},{1,9},{9,17},{17,25},{2,10},{10,18},{18,26},{... | collective-permute-start | bytes 73736 | tf_op jit(solution)/shard_map/ppermute | solution.py:25
  194.8 9.6 %collective-permute-start.19 = (f32[8,6,128]{2,0,1:T(8,128)S(1)}, f32[8,6,128]{2,0,1:T(8,128)S(1)}, u32[]{:S(2)}, u32[]{:S(2)}) collective-permute-start(f32[8,6,128]{2,0,1:T(8,128)S(1)} %get-tuple-element.49), channel_id=1, source_target_pairs={{8,0},{16,8},{24,16},{9,1},{17,9},{25,17},{10,2},{18,10},{26,18},{... | collective-permute-start | bytes 73736 | tf_op jit(solution)/shard_map/ppermute | solution.py:26
  223.7 4.5 %collective-permute-start.20 = (f32[2,2,2048]{2,1,0:T(2,128)S(1)}, f32[2,2,2048]{2,1,0:T(2,128)S(1)}, u32[]{:S(2)}, u32[]{:S(2)}) collective-permute-start(f32[2,2,2048]{2,1,0:T(2,128)S(1)} %get-tuple-element.36), channel_id=1, source_target_pairs={{0,8},{8,16},{16,24},{1,9},{9,17},{17,25},{2,10},{10,18},{18,26},{... | collective-permute-start | bytes 98312 | tf_op jit(solution)/shard_map/ppermute | solution.py:25
  226.7 10.0 %collective-permute-start.21 = (f32[2,2,2048]{2,1,0:T(2,128)S(1)}, f32[2,2,2048]{2,1,0:T(2,128)S(1)}, u32[]{:S(2)}, u32[]{:S(2)}) collective-permute-start(f32[2,2,2048]{2,1,0:T(2,128)S(1)} %get-tuple-element.37), channel_id=1, source_target_pairs={{8,0},{16,8},{24,16},{9,1},{17,9},{25,17},{10,2},{18,10},{26,18},{... | collective-permute-start | bytes 98312 | tf_op jit(solution)/shard_map/ppermute | solution.py:26
where the time goes:
time: 241 us; the launch traced here: 238 us
  waiting for transfers between devices  75.4 us (31%)
  starting transfers between devices  71.3 us (30%)
  blocking collectives  51.3 us (21%)
  local copies, waits for them, and re-layouts  17.7 us (7%)
  other arithmetic  14.9 us (6%)
  matrix products  5.12 us (2%)
    ppermute x9, waiting for transfers between devices, with_halo(): after = lax.ppermute(initial, axis, down)  67.8 us
    ppermute x9, starting transfers between devices, with_halo(): before = lax.ppermute(last, axis, up)  42 us
    all_to_all x2, blocking collectives, copy_for_each(): lax.all_to_all(jnp.broadcast_to(x[None], (peers, *x.shape)), axis, 0, 0,...  35.8 us
    all_to_all x1, blocking collectives, sum_at_owner(): lax.all_to_all(parts, axis, split_axis=0, concat_axis=0, tiled=True)  15.5 us
    gather x2, local copies, waits for them, and re-layouts, local(): picked = flat_state[obs_cell]  12.3 us
    scatter-add x2, other arithmetic, local(): jnp.zeros_like(flat_state).at[obs_cell].add(innovation).reshape(ends.shape)  11.9 us
    ppermute x9, starting transfers between devices, with_halo(): after = lax.ppermute(initial, axis, down)  11.6 us
    ppermute x4, starting transfers between devices, from_behind(): return lax.ppermute(block, axis, route)  11.1 us
  transfers between devices with their start and end apart: 23, of which 17 were waited for; matrix products, arithmetic and copies ran while one was open for 10% of the time, Pallas kernels for 0%

commit v1 on v0

v1 whole, which is shorter than its diff:
```python
import functools
import math

import jax
import jax.numpy as jnp
from jax import lax
from jax.experimental import pallas as pl
from jax.experimental.pallas import tpu as pltpu
from jax.sharding import PartitionSpec as P

MESH = pl.DeviceIdType.MESH
NV = 8
LB = 8
LANES = 128
KMAX = 6
ITERS = 2
KAPPA = 0.125
DESCENT = 0.25
KEEP = 1.0 - DESCENT
CENTER = 1.0 - 4.0 * KAPPA
GROUP = 4
F32 = jnp.float32


def start_to(src, dst, send_sem, recv_sem, mem, lat, win):
    pltpu.make_async_remote_copy(
        src_ref=src,
        dst_ref=dst,
        send_sem=send_sem,
        recv_sem=recv_sem,
        device_id={"mem": mem, "lat": lat, "win": win},
        device_id_type=MESH,
    ).start()


def drain(ref, sem):
    pltpu.make_async_copy(ref, ref, sem).wait()


def along(f, lon):
    return CENTER * f + KAPPA * (pltpu.roll(f, 1, 1) + pltpu.roll(f, lon - 1, 1))


def kernel(
    nm,
    nl,
    nw,
    e_hbm,
    c_hbm,
    d_hbm,
    coup,
    steps,
    obs_cell,
    obs_window,
    obs_value,
    obs_weight,
    err_w,
    ctl_out,
    inc_out,
    et,
    cbuf,
    sm,
    s_top,
    s_bot,
    s_in,
    r_top,
    r_bot,
    dif,
    fstate,
    bstate,
    inc_next,
    ends_own,
    ends_prev,
    wv,
    ewb,
    b1,
    ts,
    bs,
    rt,
    rb,
    pk,
    pkt,
    pkb,
    rx,
    rxt,
    rxb,
    pfull,
    ext,
    sq,
    bsum,
    o_top,
    o_bot,
    c_in,
    c_top,
    c_bot,
    local,
    e_send,
    e_recv,
    y_send,
    y_recv,
    k_send,
    k_recv,
    s_send,
    s_recv,
    d_send,
    d_recv,
    f_send,
    f_recv,
    w_send,
    w_recv,
    h_send,
    h_recv,
    o_send,
    o_recv,
):
    m, b, w = lax.axis_index("mem"), lax.axis_index("lat"), lax.axis_index("win")
    members = 2 * nm
    lon = nm * LANES
    vp = NV // nw
    scale = 1.0 / math.sqrt(members - 1)
    up, down = b > 0, b < nl - 1
    before, after = w > 0, w < nw - 1
    other = w + 1 - 2 * lax.rem(w, 2)
    planes = nw // 2
    left, right = lax.rem(m + nm - 1, nm), lax.rem(m + 1, nm)
    mine = pl.ds(pl.multiple_of(m * LANES, LANES), LANES)
    my_pair = pl.ds(2 * m, 2)
    my_piece = pl.ds(w * vp, vp)

    load_c = pltpu.make_async_copy(c_hbm.at[0], cbuf, local.at[0])
    load_c.start()
    load_d = pltpu.make_async_copy(d_hbm, dif.at[1], local.at[1])
    load_d.start()
    for i in range(vp):
        pltpu.make_async_copy(
            e_hbm.at[:, w * vp + i, :, mine], et.at[w * vp + i, my_pair], local.at[2]
        ).start()

    barrier = pltpu.get_barrier_semaphore()

    def hello(mem, lat, win):
        pl.semaphore_signal(
            barrier, inc=1, device_id={"mem": mem, "lat": lat, "win": win}, device_id_type=MESH
        )

    def greet(k, _):
        to = lax.rem(m + k, nm)

        @pl.when(k > 0)
        def _():
            hello(to, b, w)

        @pl.when(up)
        def _():
            hello(to, b - 1, w)

        @pl.when(down)
        def _():
            hello(to, b + 1, w)

        return 0

    lax.fori_loop(0, nm, greet, 0)
    for k in range(1, planes):
        hello(m, b, lax.rem(w + 2 * k, nw))
    hello(m, b, other)
    odd = lax.rem(w, 2)

    @pl.when((odd == 0) & before)
    def _():
        hello(m, b, w - 1)

    @pl.when((odd == 1) & after)
    def _():
        hello(m, b, w + 1)

    one_more = jnp.where((w > 0) & (w < nw - 1), 1, 0)
    bands = jnp.where(up, 1, 0) + jnp.where(down, 1, 0)
    pl.semaphore_wait(barrier, nm - 1 + nm * bands + planes + one_more)

    def send_e(k, _):
        to = lax.rem(m + k, nm)
        for i in range(vp):
            start_to(
                e_hbm.at[:, w * vp + i, :, pl.ds(pl.multiple_of(to * LANES, LANES), LANES)],
                et.at[w * vp + i, my_pair],
                e_send,
                e_recv,
                to,
                b,
                w,
            )
        return 0

    lax.fori_loop(1, nm, send_e, 0)

    load_c.wait()
    row8 = lax.broadcasted_iota(jnp.int32, (LB, lon), 0)
    first, last = row8 == 0, row8 == LB - 1
    edge = jnp.where(first & up, 1.0, 0.0) + jnp.where(last & down, 1.0, 0.0)
    spilled = []
    for i in range(2):
        f = cbuf[i]
        g = along(f, lon) + KAPPA * (
            jnp.where(first, 0.0, pltpu.roll(f, 1, 0)) + jnp.where(last, 0.0, pltpu.roll(f, LB - 1, 0))
        )
        e1 = KAPPA * f * edge
        sm[i] = along(g, lon) + KAPPA * (
            jnp.where(first, e1, pltpu.roll(g, 1, 0)) + jnp.where(last, e1, pltpu.roll(g, LB - 1, 0))
        )
        spilled.append((along(e1, lon) + KAPPA * g, KAPPA * e1))
    (near0, far0), (near1, far1) = spilled
    packed = jnp.where(row8 == 0, far0, pltpu.roll(near0, 1, 0))
    packed = jnp.where(row8 == 2, pltpu.roll(far1, 2, 0), packed)
    packed = jnp.where(row8 == 3, pltpu.roll(near1, 3, 0), packed)
    packed = jnp.where(row8 == 4, pltpu.roll(near0, 5, 0), packed)
    packed = jnp.where(row8 == 5, pltpu.roll(far0, 6, 0), packed)
    packed = jnp.where(row8 == 6, pltpu.roll(near1, 7, 0), packed)
    packed = jnp.where(row8 == 7, far1, packed)
    s_top[...] = packed[0:4]
    s_bot[...] = packed[4:8]
    s_in[my_pair] = sm[:, :, mine]

    def send_s(k, _):
        to = lax.rem(m + k, nm)
        cut = pl.ds(pl.multiple_of(to * LANES, LANES), LANES)

        @pl.when(k > 0)
        def _():
            start_to(sm.at[:, :, cut], s_in.at[my_pair], s_send.at[0], s_recv.at[0], to, b, w)

        @pl.when(up)
        def _():
            start_to(s_top.at[:, cut], r_bot.at[m], s_send.at[1], s_recv.at[1], to, b - 1, w)

        @pl.when(down)
        def _():
            start_to(s_bot.at[:, cut], r_top.at[m], s_send.at[2], s_recv.at[2], to, b + 1, w)

        return 0

    lax.fori_loop(0, nm, send_s, 0)

    load_d.wait()

    @pl.when(up)
    def _():
        start_to(dif.at[1], dif.at[2], d_send.at[0], d_recv.at[0], m, b - 1, w)

    @pl.when(down)
    def _():
        start_to(dif.at[1], dif.at[0], d_send.at[1], d_recv.at[1], m, b + 1, w)

    @pl.when(jnp.logical_not(up))
    def _():
        dif[0] = jnp.zeros_like(dif[0])
        r_top[...] = jnp.zeros_like(r_top)
        rt[...] = jnp.zeros_like(rt)
        rxt[...] = jnp.zeros_like(rxt)
        c_top[...] = jnp.zeros_like(c_top)
        for it in range(ITERS):
            fstate[it, 0] = jnp.zeros_like(fstate[it, 0])
            bstate[it, 0] = jnp.zeros_like(bstate[it, 0])

    @pl.when(jnp.logical_not(down))
    def _():
        dif[2] = jnp.zeros_like(dif[2])
        r_bot[...] = jnp.zeros_like(r_bot)
        rb[...] = jnp.zeros_like(rb)
        rxb[...] = jnp.zeros_like(rxb)
        c_bot[...] = jnp.zeros_like(c_bot)
        for it in range(ITERS):
            fstate[it, 2] = jnp.zeros_like(fstate[it, 2])
            bstate[it, 2] = jnp.zeros_like(bstate[it, 2])

    @pl.when(jnp.logical_not(before))
    def _():
        ends_prev[...] = jnp.zeros_like(ends_prev)

    @pl.when(jnp.logical_not(after))
    def _():
        inc_next[...] = jnp.zeros_like(inc_next)

    for v in range(NV):
        ewb[v] = jnp.full((LB, LANES), err_w[v], F32)

    tall = lax.broadcasted_iota(jnp.int32, (NV * LB, LANES), 0)
    lane_of = lax.broadcasted_iota(jnp.int32, (LANES, LANES), 0)

    def add_obs(k, total):
        at = pl.ds(k, 1)
        cell = obs_cell[at, :]
        here = (tall == lax.shift_right_logical(cell, 7)) & (obs_window[at, :] == w)
        weight = jnp.where(here, obs_weight[at, :], 0.0)
        both = jnp.concatenate([weight, weight * obs_value[at, :]], axis=0)
        hot = jnp.where(lane_of == (cell & (LANES - 1)), 1.0, 0.0)
        return total + lax.dot_general(
            both,
            hot,
            (((1,), (1,)), ((), ())),
            precision=lax.Precision.HIGHEST,
            preferred_element_type=F32,
        )

    wv[...] = lax.fori_loop(
        0, obs_cell.shape[0], add_obs, jnp.zeros((2 * NV * LB, LANES), F32)
    )

    for i in range(vp):
        drain(et.at[w * vp + i, my_pair], local.at[2])
        drain(et.at[0, pl.ds(0, members - 2)], e_recv)
    start_to(et.at[my_piece], et.at[my_piece], k_send.at[0], k_recv.at[0], m, b, other)
    order = sorted(range(1, planes), key=lambda k: -min(k, planes - k))
    for k in order:
        start_to(
            et.at[my_piece], et.at[my_piece], y_send.at[k], y_recv.at[k], m, b, lax.rem(w + 2 * k, nw)
        )
    for k in reversed(order):
        piece = et.at[pl.ds(lax.rem(w - 2 * k + nw, nw) * vp, vp)]
        drain(piece, y_recv.at[k])
        start_to(piece, piece, k_send.at[k], k_recv.at[k], m, b, other)

    drain(s_in.at[pl.ds(0, members - 2)], s_recv.at[0])

    @pl.when(up)
    def _():
        drain(r_top, s_recv.at[2])

    @pl.when(down)
    def _():
        drain(r_bot, s_recv.at[1])

    def add_spill(q, _):
        for i in range(2):
            j = 2 * q + i
            s_in[j, 0:2] = s_in[j, 0:2] + r_top[q, 2 * i : 2 * i + 2]
            s_in[j, 6:8] = s_in[j, 6:8] + r_bot[q, 2 * i : 2 * i + 2]
        return 0

    lax.fori_loop(0, nm, add_spill, 0)
    for k in range(planes):
        drain(et.at[my_piece], k_recv.at[k])

    rows24 = lax.broadcasted_iota(jnp.int32, (3 * LB, LANES), 0)
    inside24 = ((rows24 >= LB) | up) & ((rows24 < 2 * LB) | down)
    rows16 = lax.broadcasted_iota(jnp.int32, (2 * LB, LANES), 0)
    inside16 = jnp.where(((rows16 >= 4) | up) & ((rows16 < 12) | down), 1.0, 0.0)
    lane16 = lax.broadcasted_iota(jnp.int32, (2 * LB, LANES), 1)
    lane8 = lax.broadcasted_iota(jnp.int32, (LB, LANES), 1)

    def wide(ref):
        return jnp.concatenate([ref[0], ref[1], ref[2]], axis=1)

    def second(x):
        return pltpu.roll(x, 1, 1) + pltpu.roll(x, 3 * LB - 1, 1) - 2.0 * x

    def mixed(x, transposed):
        rows = []
        for v in range(NV):
            total = None
            for u in range(NV):
                term = (coup[u, v] if transposed else coup[v, u]) * x[u]
                total = term if total is None else total + term
            rows.append(total)
        return jnp.stack(rows, axis=0)

    count = jnp.full((3 * LB, LANES), steps[0], jnp.int32)

    def halo(ref, it, which):
        base = 4 * it + 2 * which

        @pl.when(up)
        def _():
            start_to(ref.at[it, 1], ref.at[it, 2], f_send.at[base], f_recv.at[base], m, b - 1, w)

        @pl.when(down)
        def _():
            start_to(ref.at[it, 1], ref.at[it, 0], f_send.at[base + 1], f_recv.at[base + 1], m, b + 1, w)

    def halo_wait(ref, it, which):
        base = 4 * it + 2 * which

        @pl.when(down)
        def _():
            drain(ref.at[it, 2], f_recv.at[base])

        @pl.when(up)
        def _():
            drain(ref.at[it, 0], f_recv.at[base + 1])

    def contract(j, total):
        return total + et[:, j] * s_in[j][None]

    for it in range(ITERS):
        if it == 0:
            total = lax.fori_loop(
                0, members, contract, jnp.zeros((NV, LB, LANES), F32), unroll=4
            )
            fstate[it, 1] = total * scale

            @pl.when(up)
            def _():
                drain(dif.at[0], d_recv.at[1])

            @pl.when(down)
            def _():
                drain(dif.at[2], d_recv.at[0])
        else:
            pfull[:, 4:12] = rx[...]
            pfull[:, 0:4] = rxt[...]
            pfull[:, 12:16] = rxb[...]

            def place(j, _):
                ext[j, 0:4] = rt[j]
                ext[j, 12:16] = rb[j]
                return 0

            lax.fori_loop(0, members, place, 0, unroll=4)

            def twice(g, total):
                f0 = ext[pl.ds(GROUP * g, GROUP)]
                sides = []
                for i in range(GROUP):
                    j = GROUP * g + i
                    from_right = pltpu.roll(pfull[1], lax.rem(LANES - 4 * j, LANES), 1)
                    from_left = pltpu.roll(pfull[0], LANES - 4 - 4 * j, 1)
                    sides.append(
                        jnp.where(lane16 < 4, from_right, jnp.where(lane16 >= LANES - 4, from_left, 0.0))
                    )
                f1 = jnp.stack(sides, axis=0)
                for _ in range(4):
                    fl0, fl1 = pltpu.roll(f0, 1, 2), pltpu.roll(f1, 1, 2)
                    fr0, fr1 = pltpu.roll(f0, LANES - 1, 2), pltpu.roll(f1, LANES - 1, 2)
                    start, end = lane16 == 0, lane16 == LANES - 1
                    n0 = (
                        jnp.where(start, fl1, fl0)
                        + jnp.where(end, fr1, fr0)
                        + pltpu.roll(f0, 1, 1)
                        + pltpu.roll(f0, 2 * LB - 1, 1)
                    )
                    n1 = (
                        jnp.where(start, fl0, fl1)
                        + jnp.where(end, fr0, fr1)
                        + pltpu.roll(f1, 1, 1)
                        + pltpu.roll(f1, 2 * LB - 1, 1)
                    )
                    f0 = (CENTER * f0 + KAPPA * n0) * inside16
                    f1 = (CENTER * f1 + KAPPA * n1) * inside16
                sq[...] = f0
                for i in range(GROUP):
                    total = total + et[:, GROUP * g + i] * sq[i, 4:12][None]
                return total

            total = lax.fori_loop(
                0, members // GROUP, twice, jnp.zeros((NV, LB, LANES), F32)
            )
            fstate[it, 1] = KEEP * fstate[it - 1, 1] - (DESCENT * scale) * total

        halo(fstate, it, 0)

        @pl.when(before)
        def _():
            start_to(
                fstate.at[it, 1], inc_next.at[it], w_send.at[2 * it], w_recv.at[2 * it], m, b, w - 1
            )

        if it == ITERS - 1:
            store_inc = pltpu.make_async_copy(fstate.at[it, 1], inc_out.at[0], local.at[3])
            store_inc.start()
        halo_wait(fstate, it, 0)
        coeff = wide(dif)

        def forth(k, u):
            moved = u + coeff * second(u) + mixed(u, False)
            moved = jnp.where(inside24, moved, 0.0)
            return jnp.where(k < count, moved, u)

        state = lax.fori_loop(0, KMAX, forth, wide(fstate.at[it]))
        ends = state[:, LB : 2 * LB]
        ends_own[it] = ends

        @pl.when(after)
        def _():
            start_to(
                ends_own.at[it],
                ends_prev.at[it],
                w_send.at[2 * it + 1],
                w_recv.at[2 * it + 1],
                m,
                b,
                w + 1,
            )

        @pl.when(after)
        def _():
            drain(inc_next.at[it], w_recv.at[2 * it])

        dense = wv[...].reshape(2, NV, LB, LANES)
        to_next = jnp.where(after, ewb[...] * (ends - inc_next[it]), 0.0)
        bstate[it, 1] = dense[0] * ends - dense[1] + to_next
        halo(bstate, it, 1)
        halo_wait(bstate, it, 1)

        def back(k, y):
            moved = y + second(coeff * y) + mixed(y, True)
            moved = jnp.where(inside24, moved, 0.0)
            return jnp.where(KMAX - 1 - k < count, moved, y)

        state = lax.fori_loop(0, KMAX, back, wide(bstate.at[it]))

        @pl.when(before)
        def _():
            drain(ends_prev.at[it], w_recv.at[2 * it + 1])

        misfit = jnp.where(before, ewb[...] * (ends_prev[it] - fstate[it, 1]), 0.0)
        gradient = (state[:, LB : 2 * LB] - misfit) * scale

        if it == 0:

            def spread(j, carry):
                lo, hi = carry
                x = jnp.sum(et[:, j] * gradient, axis=0)
                b1[j] = x
                ext[j, 4:12] = x
                ts[j] = x[0:4]
                bs[j] = x[4:8]
                here = lax.shift_right_logical(lane8, 2) == j
                lo = jnp.where(here, pltpu.roll(x, 4 * j, 1), lo)
                hi = jnp.where(here, pltpu.roll(x, lax.rem(4 * j + 4, LANES), 1), hi)
                return lo, hi

            blank = jnp.zeros((LB, LANES), F32)
            lo, hi = lax.fori_loop(0, members, spread, (blank, blank), unroll=4)
            for side, value in enumerate((lo, hi)):
                pk[side] = value
                pkt[side] = value[0:4]
                pkb[side] = value[4:8]

            @pl.when(up)
            def _():
                start_to(ts, rb, h_send.at[0], h_recv.at[0], m, b - 1, w)
                start_to(pkt.at[0], rxb.at[1], h_send.at[2], h_recv.at[2], left, b - 1, w)
                start_to(pkt.at[1], rxb.at[0], h_send.at[3], h_recv.at[3], right, b - 1, w)

            @pl.when(down)
            def _():
                start_to(bs, rt, h_send.at[1], h_recv.at[1], m, b + 1, w)
                start_to(pkb.at[0], rxt.at[1], h_send.at[4], h_recv.at[4], left, b + 1, w)
                start_to(pkb.at[1], rxt.at[0], h_send.at[5], h_recv.at[5], right, b + 1, w)

            start_to(pk.at[0], rx.at[1], h_send.at[6], h_recv.at[6], left, b, w)
            start_to(pk.at[1], rx.at[0], h_send.at[7], h_recv.at[7], right, b, w)
            drain(rx.at[1], h_recv.at[6])
            drain(rx.at[0], h_recv.at[7])

            @pl.when(down)
            def _():
                drain(rb, h_recv.at[0])
                drain(rxb.at[1], h_recv.at[2])
                drain(rxb.at[0], h_recv.at[3])

            @pl.when(up)
            def _():
                drain(rt, h_recv.at[1])
                drain(rxt.at[1], h_recv.at[4])
                drain(rxt.at[0], h_recv.at[5])
        else:

            def gather(q, _):
                for i in range(2):
                    j = 2 * q + i
                    x = jnp.sum(et[:, j] * gradient, axis=0)
                    x = (KEEP * DESCENT) * b1[j] + DESCENT * x
                    bsum[j] = x
                    o_top[q, 2 * i : 2 * i + 2] = x[0:2]
                    o_bot[q, 2 * i : 2 * i + 2] = x[6:8]
                return 0

            lax.fori_loop(0, nm, gather, 0)

    c_in[:, :, mine] = bsum[my_pair]

    def send_o(k, _):
        to = lax.rem(m + k, nm)

        @pl.when(k > 0)
        def _():
            start_to(
                bsum.at[pl.ds(2 * to, 2)], c_in.at[:, :, mine], o_send.at[0], o_recv.at[0], to, b, w
            )

        @pl.when(up)
        def _():
            start_to(o_top.at[to], c_bot.at[:, mine], o_send.at[1], o_recv.at[1], to, b - 1, w)

        @pl.when(down)
        def _():
            start_to(o_bot.at[to], c_top.at[:, mine], o_send.at[2], o_recv.at[2], to, b + 1, w)

        return 0

    lax.fori_loop(0, nm, send_o, 0)
    drain(bsum.at[pl.ds(0, members - 2)], s_send.at[0])
    drain(bsum.at[pl.ds(0, members - 2)], o_recv.at[0])

    @pl.when(down)
    def _():
        drain(s_bot, s_send.at[2])
        drain(c_bot, o_recv.at[1])

    @pl.when(up)
    def _():
        drain(s_top, s_send.at[1])
        drain(c_top, o_recv.at[2])

    packed = jnp.concatenate([c_top[...], c_bot[...]], axis=0)
    for i in range(2):
        f = c_in[i]
        near = jnp.where(
            first,
            pltpu.roll(packed, LB - (2 * i + 1), 0),
            pltpu.roll(packed, 3 - 2 * i, 0),
        )
        far = jnp.where(
            first,
            pltpu.roll(packed, (LB - 2 * i) % LB, 0) if i else packed,
            pltpu.roll(packed, 2 - 2 * i, 0) if i == 0 else packed,
        )
        g = along(f, lon) + KAPPA * (
            jnp.where(first, near, pltpu.roll(f, 1, 0)) + jnp.where(last, near, pltpu.roll(f, LB - 1, 0))
        )
        e1 = (along(near, lon) + KAPPA * (far + f)) * edge
        h = along(g, lon) + KAPPA * (
            jnp.where(first, e1, pltpu.roll(g, 1, 0)) + jnp.where(last, e1, pltpu.roll(g, LB - 1, 0))
        )
        sm[i] = (KEEP * KEEP) * cbuf[i] - h
    store_c = pltpu.make_async_copy(sm, ctl_out.at[0], local.at[4])
    store_c.start()

    for i in range(vp):
        drain(et.at[0, pl.ds(0, members - 2)], e_send)
    for k in range(planes):
        drain(et.at[my_piece], k_send.at[k])
        if k > 0:
            drain(et.at[my_piece], y_send.at[k])
    drain(bsum.at[pl.ds(0, members - 2)], o_send.at[0])

    @pl.when(up)
    def _():
        drain(dif.at[1], d_send.at[0])
        drain(o_top, o_send.at[1])
        drain(ts, h_send.at[0])
        drain(pkt.at[0], h_send.at[2])
        drain(pkt.at[1], h_send.at[3])
        for it in range(ITERS):
            drain(fstate.at[it, 1], f_send.at[4 * it])
            drain(bstate.at[it, 1], f_send.at[4 * it + 2])

    @pl.when(down)
    def _():
        drain(dif.at[1], d_send.at[1])
        drain(o_bot, o_send.at[2])
        drain(bs, h_send.at[1])
        drain(pkb.at[0], h_send.at[4])
        drain(pkb.at[1], h_send.at[5])
        for it in range(ITERS):
            drain(fstate.at[it, 1], f_send.at[4 * it + 1])
            drain(bstate.at[it, 1], f_send.at[4 * it + 3])

    drain(pk.at[0], h_send.at[6])
    drain(pk.at[1], h_send.at[7])
    for it in range(ITERS):

        @pl.when(before)
        def _():
            drain(fstate.at[it, 1], w_send.at[2 * it])

        @pl.when(after)
        def _():
            drain(ends_own.at[it], w_send.at[2 * it + 1])

    store_inc.wait()
    store_c.wait()


def local_part(nm, nl, nw, *args):
    (
        ensemble,
        weights,
        diffusivity,
        coupling,
        tl_steps,
        obs_cell,
        obs_window,
        obs_value,
        obs_weight,
        error_weight,
    ) = args
    members = 2 * nm
    lon = nm * LANES
    planes = nw // 2
    anywhere = pl.BlockSpec(memory_space=pl.ANY)
    vmem = pl.BlockSpec(memory_space=pltpu.VMEM)
    smem = pl.BlockSpec(memory_space=pltpu.SMEM)
    obs = [x.reshape(-1, LANES) for x in (obs_cell, obs_window, obs_value, obs_weight)]
    tile = (LB, LANES)
    state = (NV, *tile)
    half = (4, LANES)

    def buf(*shape):
        return pltpu.VMEM(shape, F32)

    dma = pltpu.SemaphoreType.DMA
    return pl.pallas_call(
        functools.partial(kernel, nm, nl, nw),
        name="assimilate",
        out_shape=(
            jax.ShapeDtypeStruct((1, 2, LB, lon), F32),
            jax.ShapeDtypeStruct((1, *state), F32),
        ),
        in_specs=[anywhere, anywhere, anywhere, smem, smem, vmem, vmem, vmem, vmem, smem],
        out_specs=(anywhere, anywhere),
        scratch_shapes=[
            buf(NV, members, *tile),
            buf(2, LB, lon),
            buf(2, LB, lon),
            buf(4, lon),
            buf(4, lon),
            buf(members, *tile),
            buf(nm, *half),
            buf(nm, *half),
            buf(3, *state),
            buf(ITERS, 3, *state),
            buf(ITERS, 3, *state),
            buf(ITERS, *state),
            buf(ITERS, *state),
            buf(ITERS, *state),
            buf(2 * NV * LB, LANES),
            buf(*state),
            buf(members, *tile),
            buf(members, *half),
            buf(members, *half),
            buf(members, *half),
            buf(members, *half),
            buf(2, *tile),
            buf(2, *half),
            buf(2, *half),
            buf(2, *tile),
            buf(2, *half),
            buf(2, *half),
            buf(2, 2 * LB, LANES),
            buf(members, 2 * LB, LANES),
            buf(GROUP, 2 * LB, LANES),
            buf(members, *tile),
            buf(nm, *half),
            buf(nm, *half),
            buf(2, LB, lon),
            buf(4, lon),
            buf(4, lon),
            dma((5,)),
            dma,
            dma,
            dma((planes,)),
            dma((planes,)),
            dma((planes,)),
            dma((planes,)),
            dma((3,)),
            dma((3,)),
            dma((2,)),
            dma((2,)),
            dma((4 * ITERS,)),
            dma((4 * ITERS,)),
            dma((2 * ITERS,)),
            dma((2 * ITERS,)),
            dma((8,)),
            dma((8,)),
            dma((3,)),
            dma((3,)),
        ],
        compiler_params=pltpu.CompilerParams(
            collective_id=0, has_side_effects=True, vmem_limit_bytes=40 * 1024 * 1024
        ),
    )(
        ensemble,
        weights,
        diffusivity,
        coupling,
        tl_steps,
        *obs,
        error_weight,
    )


def solution(mesh):
    sizes = [mesh.shape[axis] for axis in ("mem", "lat", "win")]
    return jax.shard_map(
        functools.partial(local_part, *sizes),
        mesh=mesh,
        in_specs=(
            P("mem", None, "lat", None),
            P("win", "mem", "lat", None),
            P(None, "lat", "mem"),
            P(),
            P("win"),
            P(("mem", "lat")),
            P(("mem", "lat")),
            P(("mem", "lat")),
            P(("mem", "lat")),
            P(),
        ),
        out_specs=(P("win", "mem", "lat", None), P("win", None, "lat", "mem")),
        check_vma=False,
    )
```

time: 241 us -> 89.5 us (0.37)
  the two profiles are of different devices: /device:TPU:24 before, /device:TPU:2 now
where the time goes in v1:
time: 89.5 us; the launch traced here: 89.1 us
  Pallas kernels  80.9 us (90%)
  local copies, waits for them, and re-layouts  6.89 us (8%)
  between operations  1.34 us (1%)
    pallas_call x1, Pallas kernels, local_part(): pl.pallas_call(functools.partial(kernel, nm, nl, nw), name='assimilate',...  80.9 us
    unnamed x20, local copies, waits for them, and re-layouts  6.89 us

profile of v1, /device:TPU:2, one launch (start us, length us, event | category | flops | bytes accessed | tf_op | source)
XLA Modules:
  0.0 89.1 jit_solution(2597869923375185741)
XLA Ops:
  0.6 0.0 copy-start.4
  1.3 0.0 copy-start.3
  1.3 0.0 copy-start.8
  1.3 0.0 copy-done.4
  1.3 0.7 copy-done.3
  2.0 0.0 copy-done.8
  2.0 0.0 copy-start
  2.0 1.2 %copy-done = f32[2,8,8,2048]{3,2,1,0:T(8,128)S(1)} copy-done((f32[2,8,8,2048]{3,2,1,0:T(8,128)S(1)}, f32[2,8,8,2048]{3,2,1,0:T(8,128)}, u32[]{:S(2)}) %copy-start) | copy-done | bytes 1048600
  3.2 0.0 copy-start.1
  3.2 0.9 %copy-done.1 = f32[1,2,8,2048]{3,2,1,0:T(8,128)S(1)} copy-done((f32[1,2,8,2048]{3,2,1,0:T(8,128)S(1)}, f32[1,2,8,2048]{3,2,1,0:T(8,128)}, u32[]{:S(2)}) %copy-start.1) | copy-done | bytes 131096
  4.1 0.0 copy-start.2
  4.1 0.8 copy-done.2
  4.9 0.0 copy-start.5
  4.9 0.7 copy-done.5
  5.6 0.0 copy-start.6
  5.6 0.7 copy-done.6
  6.3 0.0 copy-start.7
  6.3 0.7 copy-done.7
  6.9 80.9 %assimilate.1 = (f32[1,2,8,2048]{3,2,1,0:T(8,128)S(1)}, f32[1,8,8,128]{3,2,1,0:T(8,128)S(1)}) custom-call(f32[2,8,8,2048]{3,2,1,0:T(8,128)S(1)} %copy-done, f32[1,2,8,2048]{3,2,1,0:T(8,128)S(1)} %copy-done.1, f32[8,8,128]{2,1,0:T(8,128)S(1)} %copy-done.2, f32[8,8]{1,0:T(8,128)S(1)} %copy-done.3, s32[1]{0:T(128)S(6)} %copy.14.steps, s32[8,128]{1,0:T(8,128)S(1)} %bitcast.4, ...), custom_call_target="tpu_custom_call" | custom-call | tf_op jit(solution)/shard_map/assimilate/pallas_call | solution.py:714
  87.8 0.7 copy.15
  88.5 0.6 copy.16
Async XLA Ops:
  0.6 0.7 copy-start.4
  1.3 0.7 copy-start.3
  1.3 0.7 copy-start.8
  2.0 1.2 %copy-start = (f32[2,8,8,2048]{3,2,1,0:T(8,128)S(1)}, f32[2,8,8,2048]{3,2,1,0:T(8,128)}, u32[]{:S(2)}) copy-start(f32[2,8,8,2048]{3,2,1,0:T(8,128)} %e_hbm.1) | copy-start | bytes 3145732
  3.2 0.9 %copy-start.1 = (f32[1,2,8,2048]{3,2,1,0:T(8,128)S(1)}, f32[1,2,8,2048]{3,2,1,0:T(8,128)}, u32[]{:S(2)}) copy-start(f32[1,2,8,2048]{3,2,1,0:T(8,128)} %c_hbm.1) | copy-start | bytes 393220
  4.1 0.8 copy-start.2
  4.9 0.7 copy-start.5
  5.6 0.7 copy-start.6
  6.3 0.7 copy-start.7

commit v2 on v1

v2 whole, which is shorter than its diff:
```python
import functools
import math

import jax
import jax.numpy as jnp
from jax import lax
from jax.experimental import pallas as pl
from jax.experimental.pallas import tpu as pltpu
from jax.sharding import PartitionSpec as P

MESH = pl.DeviceIdType.MESH
NV = 8
LB = 8
LANES = 128
KMAX = 6
ITERS = 2
KAPPA = 0.125
DESCENT = 0.25
KEEP = 1.0 - DESCENT
CENTER = 1.0 - 4.0 * KAPPA
F32 = jnp.float32


def start_to(src, dst, send_sem, recv_sem, mem, lat, win):
    pltpu.make_async_remote_copy(
        src_ref=src,
        dst_ref=dst,
        send_sem=send_sem,
        recv_sem=recv_sem,
        device_id={"mem": mem, "lat": lat, "win": win},
        device_id_type=MESH,
    ).start()


def drain(ref, sem):
    pltpu.make_async_copy(ref, ref, sem).wait()


def along(f, lon):
    return CENTER * f + KAPPA * (pltpu.roll(f, 1, 1) + pltpu.roll(f, lon - 1, 1))


def kernel(
    nm,
    nl,
    nw,
    e_hbm,
    c_hbm,
    d_hbm,
    coup_hbm,
    steps,
    obs0,
    obs1,
    obs2,
    obs3,
    err_hbm,
    ctl_out,
    inc_out,
    coup,
    err_w,
    obs_cell,
    obs_window,
    obs_value,
    obs_weight,
    et,
    cbuf,
    sm,
    s_top,
    s_bot,
    s_in,
    r_top,
    r_bot,
    dif,
    fstate,
    bstate,
    inc_next,
    ends_own,
    ends_prev,
    wv,
    ewb,
    e_up,
    e_down,
    eh,
    b1,
    bh,
    b_up,
    b_down,
    r_far,
    pk,
    rx,
    rxc,
    sq,
    obuf,
    c_in,
    local,
    e_send,
    e_recv,
    y_send,
    y_recv,
    k_send,
    k_recv,
    s_send,
    s_recv,
    d_send,
    d_recv,
    f_send,
    f_recv,
    w_send,
    w_recv,
    g_send,
    g_recv,
    y2_send,
    y2_recv,
    k2_send,
    k2_recv,
    h_send,
    h_recv,
    o_send,
    o_recv,
):
    m, b, w = lax.axis_index("mem"), lax.axis_index("lat"), lax.axis_index("win")
    members = 2 * nm
    lon = nm * LANES
    vp = NV // nw
    scale = 1.0 / math.sqrt(members - 1)
    up, down = b > 0, b < nl - 1
    before, after = w > 0, w < nw - 1
    other = w + 1 - 2 * lax.rem(w, 2)
    planes = nw // 2
    groups = members // LB
    left, right = lax.rem(m + nm - 1, nm), lax.rem(m + 1, nm)
    mine = pl.ds(pl.multiple_of(m * LANES, LANES), LANES)
    my_pair = pl.ds(2 * m, 2)
    my_piece = pl.ds(w * vp, vp)

    load_c = pltpu.make_async_copy(c_hbm.at[0], cbuf, local.at[0])
    load_c.start()
    load_d = pltpu.make_async_copy(d_hbm, dif.at[1], local.at[1])
    load_d.start()
    small = [
        pltpu.make_async_copy(src, dst, local.at[5 + i])
        for i, (src, dst) in enumerate(
            (
                (coup_hbm, coup),
                (err_hbm, err_w),
                (obs0, obs_cell),
                (obs1, obs_window),
                (obs2, obs_value),
                (obs3, obs_weight),
            )
        )
    ]
    for copy in small:
        copy.start()
    for i in range(vp):
        pltpu.make_async_copy(
            e_hbm.at[:, w * vp + i, :, mine], et.at[w * vp + i, my_pair], local.at[2]
        ).start()

    barrier = pltpu.get_barrier_semaphore()

    def hello(mem, lat, win):
        pl.semaphore_signal(
            barrier, inc=1, device_id={"mem": mem, "lat": lat, "win": win}, device_id_type=MESH
        )

    def greet(k, _):
        to = lax.rem(m + k, nm)

        @pl.when(k > 0)
        def _():
            hello(to, b, w)

        @pl.when(up)
        def _():
            hello(to, b - 1, w)

        @pl.when(down)
        def _():
            hello(to, b + 1, w)

        return 0

    lax.fori_loop(0, nm, greet, 0)
    for k in range(1, planes):
        hello(m, b, lax.rem(w + 2 * k, nw))
    hello(m, b, other)
    odd = lax.rem(w, 2)

    @pl.when((odd == 0) & before)
    def _():
        hello(m, b, w - 1)

    @pl.when((odd == 1) & after)
    def _():
        hello(m, b, w + 1)

    one_more = jnp.where((w > 0) & (w < nw - 1), 1, 0)
    bands = jnp.where(up, 1, 0) + jnp.where(down, 1, 0)
    pl.semaphore_wait(barrier, nm - 1 + nm * bands + planes + one_more)

    def send_e(k, _):
        to = lax.rem(m + k, nm)
        for i in range(vp):
            start_to(
                e_hbm.at[:, w * vp + i, :, pl.ds(pl.multiple_of(to * LANES, LANES), LANES)],
                et.at[w * vp + i, my_pair],
                e_send,
                e_recv,
                to,
                b,
                w,
            )
        return 0

    lax.fori_loop(1, nm, send_e, 0)

    load_c.wait()
    row8 = lax.broadcasted_iota(jnp.int32, (LB, lon), 0)
    first, last = row8 == 0, row8 == LB - 1
    edge = jnp.where(first & up, 1.0, 0.0) + jnp.where(last & down, 1.0, 0.0)
    spilled = []
    for i in range(2):
        f = cbuf[i]
        g = along(f, lon) + KAPPA * (
            jnp.where(first, 0.0, pltpu.roll(f, 1, 0)) + jnp.where(last, 0.0, pltpu.roll(f, LB - 1, 0))
        )
        e1 = KAPPA * f * edge
        sm[i] = along(g, lon) + KAPPA * (
            jnp.where(first, e1, pltpu.roll(g, 1, 0)) + jnp.where(last, e1, pltpu.roll(g, LB - 1, 0))
        )
        spilled.append((along(e1, lon) + KAPPA * g, KAPPA * e1))
    (near0, far0), (near1, far1) = spilled
    packed = jnp.where(row8 == 0, far0, pltpu.roll(near0, 1, 0))
    packed = jnp.where(row8 == 2, pltpu.roll(far1, 2, 0), packed)
    packed = jnp.where(row8 == 3, pltpu.roll(near1, 3, 0), packed)
    packed = jnp.where(row8 == 4, pltpu.roll(near0, 5, 0), packed)
    packed = jnp.where(row8 == 5, pltpu.roll(far0, 6, 0), packed)
    packed = jnp.where(row8 == 6, pltpu.roll(near1, 7, 0), packed)
    packed = jnp.where(row8 == 7, far1, packed)
    s_top[...] = packed[0:4]
    s_bot[...] = packed[4:8]
    s_in[my_pair] = sm[:, :, mine]

    def send_s(k, _):
        to = lax.rem(m + k, nm)
        cut = pl.ds(pl.multiple_of(to * LANES, LANES), LANES)

        @pl.when(up)
        def _():
            start_to(s_top.at[:, cut], r_bot.at[m], s_send.at[1], s_recv.at[1], to, b - 1, w)

        @pl.when(down)
        def _():
            start_to(s_bot.at[:, cut], r_top.at[m], s_send.at[2], s_recv.at[2], to, b + 1, w)

        return 0

    def send_s_own(k, _):
        to = lax.rem(m + k, nm)
        cut = pl.ds(pl.multiple_of(to * LANES, LANES), LANES)
        start_to(sm.at[:, :, cut], s_in.at[my_pair], s_send.at[0], s_recv.at[0], to, b, w)
        return 0

    lax.fori_loop(0, nm, send_s, 0)
    lax.fori_loop(1, nm, send_s_own, 0)

    @pl.when(jnp.logical_not(up))
    def _():
        dif[0] = jnp.zeros_like(dif[0])
        r_top[...] = jnp.zeros_like(r_top)
        r_far[0] = jnp.zeros_like(r_far[0])
        rxc[0] = jnp.zeros_like(rxc[0])
        for i in range(vp):
            eh[w * vp + i, 0] = jnp.zeros_like(r_far[0])
        for it in range(ITERS):
            fstate[it, 0] = jnp.zeros_like(fstate[it, 0])
            bstate[it, 0] = jnp.zeros_like(bstate[it, 0])

    @pl.when(jnp.logical_not(down))
    def _():
        dif[2] = jnp.zeros_like(dif[2])
        r_bot[...] = jnp.zeros_like(r_bot)
        r_far[1] = jnp.zeros_like(r_far[1])
        rxc[1] = jnp.zeros_like(rxc[1])
        for i in range(vp):
            eh[w * vp + i, 1] = jnp.zeros_like(r_far[1])
        for it in range(ITERS):
            fstate[it, 2] = jnp.zeros_like(fstate[it, 2])
            bstate[it, 2] = jnp.zeros_like(bstate[it, 2])

    @pl.when(jnp.logical_not(before))
    def _():
        ends_prev[...] = jnp.zeros_like(ends_prev)

    @pl.when(jnp.logical_not(after))
    def _():
        inc_next[...] = jnp.zeros_like(inc_next)

    for copy in small:
        copy.wait()
    for v in range(NV):
        ewb[v] = jnp.full((LB, LANES), err_w[v], F32)

    tall = lax.broadcasted_iota(jnp.int32, (NV * LB, LANES), 0)
    lane_of = lax.broadcasted_iota(jnp.int32, (LANES, LANES), 0)

    def add_obs(k, total):
        at = pl.ds(k, 1)
        cell = obs_cell[at, :]
        here = (tall == lax.shift_right_logical(cell, 7)) & (obs_window[at, :] == w)
        weight = jnp.where(here, obs_weight[at, :], 0.0)
        both = jnp.concatenate([weight, weight * obs_value[at, :]], axis=0)
        hot = jnp.where(lane_of == (cell & (LANES - 1)), 1.0, 0.0)
        return total + lax.dot_general(
            both,
            hot,
            (((1,), (1,)), ((), ())),
            precision=lax.Precision.HIGHEST,
            preferred_element_type=F32,
        )

    wv[...] = lax.fori_loop(
        0, obs_cell.shape[0], add_obs, jnp.zeros((2 * NV * LB, LANES), F32)
    )

    for i in range(vp):
        drain(et.at[w * vp + i, my_pair], local.at[2])
        drain(et.at[0, pl.ds(0, members - 2)], e_recv)
    start_to(et.at[my_piece], et.at[my_piece], k_send.at[0], k_recv.at[0], m, b, other)
    order = sorted(range(1, planes), key=lambda k: -min(k, planes - k))
    for k in order:
        start_to(
            et.at[my_piece], et.at[my_piece], y_send.at[k], y_recv.at[k], m, b, lax.rem(w + 2 * k, nw)
        )
    drain(s_in.at[pl.ds(0, members - 2)], s_recv.at[0])

    @pl.when(up)
    def _():
        drain(r_top, s_recv.at[2])

    @pl.when(down)
    def _():
        drain(r_bot, s_recv.at[1])

    def add_spill(q, _):
        for i in range(2):
            j = 2 * q + i
            s_in[j, 0:2] = s_in[j, 0:2] + r_top[q, 2 * i : 2 * i + 2]
            s_in[j, 6:8] = s_in[j, 6:8] + r_bot[q, 2 * i : 2 * i + 2]
        return 0

    lax.fori_loop(0, nm, add_spill, 0)
    load_d.wait()

    @pl.when(up)
    def _():
        start_to(dif.at[1], dif.at[2], d_send.at[0], d_recv.at[0], m, b - 1, w)

    @pl.when(down)
    def _():
        start_to(dif.at[1], dif.at[0], d_send.at[1], d_recv.at[1], m, b + 1, w)

    def first_increment(v):
        fstate[0, 1, v] = jnp.sum(et[v] * s_in[...], axis=0) * scale

    for i in range(vp):
        v = w * vp + i
        for j in range(members):
            e_up[2 * j : 2 * j + 2, :] = et[v, j, 0:2]
            e_down[2 * j : 2 * j + 2, :] = et[v, j, 6:8]

        @pl.when(up)
        def _():
            start_to(e_up, eh.at[v, 1], g_send.at[0], g_recv.at[0], m, b - 1, w)

        @pl.when(down)
        def _():
            start_to(e_down, eh.at[v, 0], g_send.at[1], g_recv.at[1], m, b + 1, w)

        if i < vp - 1:

            @pl.when(up)
            def _():
                drain(e_up, g_send.at[0])

            @pl.when(down)
            def _():
                drain(e_down, g_send.at[1])

        first_increment(v)

    for k in reversed(order):
        origin = lax.rem(w - 2 * k + nw, nw) * vp
        piece = et.at[pl.ds(origin, vp)]
        drain(piece, y_recv.at[k])
        start_to(piece, piece, k_send.at[k], k_recv.at[k], m, b, other)
        for i in range(vp):
            first_increment(origin + i)
    for k in [0, *reversed(order)]:
        origin = lax.rem(other - 2 * k + nw, nw) * vp
        drain(et.at[pl.ds(origin, vp)], k_recv.at[k])
        for i in range(vp):
            first_increment(origin + i)

    rows24 = lax.broadcasted_iota(jnp.int32, (3 * LB, LANES), 0)
    inside24 = ((rows24 >= LB) | up) & ((rows24 < 2 * LB) | down)
    lane = lax.broadcasted_iota(jnp.int32, (LB, LANES), 1)
    row = lax.broadcasted_iota(jnp.int32, (LB, LANES), 0)
    up_f = jnp.where(up, 1.0, 0.0)
    down_f = jnp.where(down, 1.0, 0.0)

    def wide(ref):
        return jnp.concatenate([ref[0], ref[1], ref[2]], axis=1)

    def second(x):
        return pltpu.roll(x, 1, 1) + pltpu.roll(x, 3 * LB - 1, 1) - 2.0 * x

    def mixed(x, transposed):
        rows = []
        for v in range(NV):
            total = None
            for u in range(NV):
                term = (coup[u, v] if transposed else coup[v, u]) * x[u]
                total = term if total is None else total + term
            rows.append(total)
        return jnp.stack(rows, axis=0)

    count = jnp.full((3 * LB, LANES), steps[0], jnp.int32)

    def halo(ref, it, which):
        base = 4 * it + 2 * which

        @pl.when(up)
        def _():
            start_to(ref.at[it, 1], ref.at[it, 2], f_send.at[base], f_recv.at[base], m, b - 1, w)

        @pl.when(down)
        def _():
            start_to(ref.at[it, 1], ref.at[it, 0], f_send.at[base + 1], f_recv.at[base + 1], m, b + 1, w)

    def halo_wait(ref, it, which):
        base = 4 * it + 2 * which

        @pl.when(down)
        def _():
            drain(ref.at[it, 2], f_recv.at[base])

        @pl.when(up)
        def _():
            drain(ref.at[it, 0], f_recv.at[base + 1])

    my_edges = eh.at[my_piece]

    def send_edges():
        for i in range(vp):

            @pl.when(down)
            def _():
                drain(eh.at[0, 1], g_recv.at[0])

            @pl.when(up)
            def _():
                drain(eh.at[0, 0], g_recv.at[1])

        start_to(my_edges, my_edges, k2_send.at[0], k2_recv.at[0], m, b, other)
        for k in order:
            start_to(my_edges, my_edges, y2_send.at[k], y2_recv.at[k], m, b, lax.rem(w + 2 * k, nw))

    def pass_edges():
        for k in reversed(order):
            piece = eh.at[pl.ds(lax.rem(w - 2 * k + nw, nw) * vp, vp)]
            drain(piece, y2_recv.at[k])
            start_to(piece, piece, k2_send.at[k], k2_recv.at[k], m, b, other)

    def rows_of(ref, first_row, stride, g):
        return ref[pl.ds(g * LB * stride + first_row, LB, stride=stride), :]

    def beside(x, y, to_left):
        shift, end = (1, lane == 0) if to_left else (LANES - 1, lane == LANES - 1)
        return jnp.where(end, pltpu.roll(y, shift, 2), pltpu.roll(x, shift, 2))

    def masked(x, depth):
        n = x.shape[0]
        return jnp.concatenate([x[:depth] * up_f, x[depth : n - depth], x[n - depth :] * down_f], axis=0)

    def smooth_group(g):
        main = [r_far[0, pl.ds(2 * LB * g + r, LB, stride=2), :] for r in range(2)]
        main += [bh[0, pl.ds(2 * LB * g + r, LB, stride=2), :] for r in range(2)]
        main += [rows_of(b1, r, LB, g) for r in range(LB)]
        main += [bh[1, pl.ds(2 * LB * g + r, LB, stride=2), :] for r in range(2)]
        main += [r_far[1, pl.ds(2 * LB * g + r, LB, stride=2), :] for r in range(2)]
        places = [(rxc, 0, 4), (rxc, 0, 5), (rx, 1, 0), (rx, 1, 1)]
        places += [(rx, 0, r) for r in range(LB)]
        places += [(rx, 1, 2), (rx, 1, 3), (rxc, 1, 2), (rxc, 1, 3)]
        sides = []
        for ref, which, r in places:
            at = 4 * (groups * r + g)
            lo, hi = (ref[which, 0], ref[which, 1]) if ref is rxc else (ref[0, which], ref[1, which])
            from_left = pltpu.roll(lo, LANES - 4 - at, 1)
            from_right = pltpu.roll(hi, (LANES - at) % LANES, 1)
            sides.append(jnp.where(lane < 4, from_right, jnp.where(lane >= LANES - 4, from_left, 0.0)))
        f0, f1 = jnp.stack(main, axis=0), jnp.stack(sides, axis=0)
        for depth in (3, 2, 1, 0):
            m0, m1 = f0[1:-1], f1[1:-1]
            n0 = beside(m0, m1, True) + beside(m0, m1, False) + f0[2:] + f0[:-2]
            n1 = beside(m1, m0, True) + beside(m1, m0, False) + f1[2:] + f1[:-2]
            f0 = CENTER * m0 + KAPPA * n0
            f1 = CENTER * m1 + KAPPA * n1
            if depth:
                f0, f1 = masked(f0, depth), masked(f1, depth)
        for r in range(LB):
            sq[pl.ds(LB * LB * g + r, LB, stride=LB), :] = f0[r]

    def member_rows(j):
        return pl.ds(pl.multiple_of(LB * j, LB), LB)

    def fourfold(x, from_row):
        x = jnp.where((row == from_row) | (row == from_row + 1), x, 0.0)
        x = x + pltpu.roll(x, 2, 1)
        return x + pltpu.roll(x, 4, 1)

    def edge_rows(gradient):
        out = []
        for side, part in enumerate((gradient[:, :LB], gradient[:, 2 * LB :])):
            tile = fourfold(part, 0 if side else LB - 2)
            rows = eh[:, side].reshape(NV, groups * 2, LB, LANES)
            out.append(jnp.sum(rows * tile[:, None], axis=0).reshape(2 * members, LANES))
        return out

    for it in range(ITERS):
        if it > 0:
            total = jnp.zeros((NV, LB, LANES), F32)
            drain(rx.at[1], h_recv.at[0])
            drain(rx.at[0], h_recv.at[1])

            @pl.when(down)
            def _():
                drain(rxc.at[1, 1], h_recv.at[2])
                drain(rxc.at[1, 0], h_recv.at[3])

            @pl.when(up)
            def _():
                drain(rxc.at[0, 1], h_recv.at[4])
                drain(rxc.at[0, 0], h_recv.at[5])

            def add_member(j, total):
                return total + et[:, j] * sq[member_rows(j), :][None]

            for g in range(groups):
                part = pl.ds(2 * LB * g, 2 * LB)

                @pl.when(down)
                def _():
                    drain(r_far.at[1, part], h_recv.at[6 + 2 * g])

                @pl.when(up)
                def _():
                    drain(r_far.at[0, part], h_recv.at[7 + 2 * g])

                smooth_group(g)
                total = lax.fori_loop(LB * g, LB * (g + 1), add_member, total, unroll=True)
            fstate[it, 1] = KEEP * fstate[it - 1, 1] - (DESCENT * scale) * total

        halo(fstate, it, 0)

        @pl.when(before)
        def _():
            start_to(
                fstate.at[it, 1], inc_next.at[it], w_send.at[2 * it], w_recv.at[2 * it], m, b, w - 1
            )

        if it == ITERS - 1:
            inc_out[0] = fstate[it, 1]
        else:
            send_edges()

            @pl.when(up)
            def _():
                drain(dif.at[0], d_recv.at[1])

            @pl.when(down)
            def _():
                drain(dif.at[2], d_recv.at[0])

        halo_wait(fstate, it, 0)
        coeff = wide(dif)

        def forth(k, u):
            moved = u + coeff * second(u) + mixed(u, False)
            moved = jnp.where(inside24, moved, 0.0)
            return jnp.where(k < count, moved, u)

        state = lax.fori_loop(0, KMAX, forth, wide(fstate.at[it]))
        ends = state[:, LB : 2 * LB]
        for part in range(3):
            ends_own[it, part] = state[:, LB * part : LB * (part + 1)]

        @pl.when(after)
        def _():
            start_to(
                ends_own.at[it],
                ends_prev.at[it],
                w_send.at[2 * it + 1],
                w_recv.at[2 * it + 1],
                m,
                b,
                w + 1,
            )

        @pl.when(after)
        def _():
            drain(inc_next.at[it], w_recv.at[2 * it])

        dense = wv[...].reshape(2, NV, LB, LANES)
        to_next = jnp.where(after, ewb[...] * (ends - inc_next[it]), 0.0)
        bstate[it, 1] = dense[0] * ends - dense[1] + to_next
        halo(bstate, it, 1)
        if it == 0:
            pass_edges()
        halo_wait(bstate, it, 1)

        def back(k, y):
            moved = y + second(coeff * y) + mixed(y, True)
            moved = jnp.where(inside24, moved, 0.0)
            return jnp.where(KMAX - 1 - k < count, moved, y)

        state = lax.fori_loop(0, KMAX, back, wide(bstate.at[it]))

        @pl.when(before)
        def _():
            drain(ends_prev.at[it], w_recv.at[2 * it + 1])

        wide_w = jnp.concatenate([ewb[...]] * 3, axis=1)
        misfit = jnp.where(before, wide_w * (wide(ends_prev.at[it]) - wide(fstate.at[it])), 0.0)
        gradient = (state - misfit) * scale
        own = gradient[:, LB : 2 * LB]

        if it == 0:

            def spread(j, _):
                b1[member_rows(j), :] = jnp.sum(et[:, j] * own, axis=0)
                return 0

            lax.fori_loop(0, members, spread, 0, unroll=4)
            for g in range(groups):
                for r in range(2):
                    to_row = pl.ds(2 * LB * g + r, LB, stride=2)
                    b_up[to_row, :] = rows_of(b1, 2 + r, LB, g)
                    b_down[to_row, :] = rows_of(b1, 4 + r, LB, g)

            for k in range(planes):
                drain(my_edges, k2_recv.at[k])
            top, bottom = edge_rows(gradient)
            bh[0] = top
            bh[1] = bottom
            for part in range(2):
                lo = hi = jnp.zeros((LB, LANES), F32)
                for r in range(LB if part == 0 else 4):
                    for g in range(groups):
                        if part == 0:
                            x = rows_of(b1, r, LB, g)
                        else:
                            x = bh[r // 2, pl.ds(2 * LB * g + r % 2, LB, stride=2), :]
                        at = groups * r + g
                        here = lax.shift_right_logical(lane, 2) == at
                        lo = jnp.where(here, pltpu.roll(x, 4 * at, 1) if at else x, lo)
                        hi = jnp.where(here, pltpu.roll(x, (4 * at + 4) % LANES, 1), hi)
                pk[0, part] = lo
                pk[1, part] = hi

            @pl.when(up)
            def _():
                start_to(pk.at[0, 0], rxc.at[1, 1], h_send.at[2], h_recv.at[2], left, b - 1, w)
                start_to(pk.at[1, 0], rxc.at[1, 0], h_send.at[3], h_recv.at[3], right, b - 1, w)

            @pl.when(down)
            def _():
                start_to(pk.at[0, 0], rxc.at[0, 1], h_send.at[4], h_recv.at[4], left, b + 1, w)
                start_to(pk.at[1, 0], rxc.at[0, 0], h_send.at[5], h_recv.at[5], right, b + 1, w)

            start_to(pk.at[0], rx.at[1], h_send.at[0], h_recv.at[0], left, b, w)
            start_to(pk.at[1], rx.at[0], h_send.at[1], h_recv.at[1], right, b, w)
            for g in range(groups):
                part = pl.ds(2 * LB * g, 2 * LB)

                @pl.when(up)
                def _():
                    start_to(
                        b_up.at[part], r_far.at[1, part], h_send.at[6 + 2 * g], h_recv.at[6 + 2 * g], m, b - 1, w
                    )

                @pl.when(down)
                def _():
                    start_to(
                        b_down.at[part], r_far.at[0, part], h_send.at[7 + 2 * g], h_recv.at[7 + 2 * g], m, b + 1, w
                    )
        else:

            def gather(q, _):
                for i in range(2):
                    j = 2 * q + i
                    x = jnp.sum(et[:, j] * own, axis=0)
                    obuf[q, i] = (KEEP * DESCENT) * b1[member_rows(j), :] + DESCENT * x
                return 0

            lax.fori_loop(0, nm, gather, 0, unroll=2)
            top, bottom = edge_rows(gradient)
            top = (KEEP * DESCENT) * bh[0] + DESCENT * top
            bottom = (KEEP * DESCENT) * bh[1] + DESCENT * bottom
            for q in range(nm):
                obuf[q, 2, 0:4] = top[4 * q : 4 * q + 4]
                obuf[q, 2, 4:8] = bottom[4 * q : 4 * q + 4]

    c_in[:, :, mine] = obuf[m]

    def send_o(k, _):
        to = lax.rem(m + k, nm)
        start_to(obuf.at[to], c_in.at[:, :, mine], o_send, o_recv, to, b, w)
        return 0

    lax.fori_loop(1, nm, send_o, 0)
    drain(obuf.at[pl.ds(0, nm - 1)], o_recv)
    packed = c_in[2]
    for i in range(2):
        f = c_in[i]
        near = jnp.where(
            first,
            pltpu.roll(packed, LB - (2 * i + 1), 0),
            pltpu.roll(packed, 3 - 2 * i, 0),
        )
        far = jnp.where(
            first,
            pltpu.roll(packed, (LB - 2 * i) % LB, 0) if i else packed,
            pltpu.roll(packed, 2 - 2 * i, 0) if i == 0 else packed,
        )
        g = along(f, lon) + KAPPA * (
            jnp.where(first, near, pltpu.roll(f, 1, 0)) + jnp.where(last, near, pltpu.roll(f, LB - 1, 0))
        )
        e1 = (along(near, lon) + KAPPA * (far + f)) * edge
        h = along(g, lon) + KAPPA * (
            jnp.where(first, e1, pltpu.roll(g, 1, 0)) + jnp.where(last, e1, pltpu.roll(g, LB - 1, 0))
        )
        ctl_out[0, i] = (KEEP * KEEP) * cbuf[i] - h

    for i in range(vp):
        drain(et.at[0, pl.ds(0, members - 2)], e_send)
    for k in range(planes):
        drain(et.at[my_piece], k_send.at[k])
        drain(my_edges, k2_send.at[k])
        if k > 0:
            drain(et.at[my_piece], y_send.at[k])
            drain(my_edges, y2_send.at[k])
    drain(s_in.at[pl.ds(0, members - 2)], s_send.at[0])
    drain(obuf.at[pl.ds(0, nm - 1)], o_send)

    @pl.when(up)
    def _():
        drain(s_top, s_send.at[1])
        drain(dif.at[1], d_send.at[0])
        drain(e_up, g_send.at[0])
        drain(pk.at[0, 0], h_send.at[2])
        drain(pk.at[1, 0], h_send.at[3])
        for it in range(ITERS):
            drain(fstate.at[it, 1], f_send.at[4 * it])
            drain(bstate.at[it, 1], f_send.at[4 * it + 2])

    @pl.when(down)
    def _():
        drain(s_bot, s_send.at[2])
        drain(dif.at[1], d_send.at[1])
        drain(e_down, g_send.at[1])
        drain(pk.at[0, 0], h_send.at[4])
        drain(pk.at[1, 0], h_send.at[5])
        for it in range(ITERS):
            drain(fstate.at[it, 1], f_send.at[4 * it + 1])
            drain(bstate.at[it, 1], f_send.at[4 * it + 3])

    drain(pk.at[0], h_send.at[0])
    drain(pk.at[1], h_send.at[1])
    for g in range(groups):
        part = pl.ds(2 * LB * g, 2 * LB)

        @pl.when(up)
        def _():
            drain(b_up.at[part], h_send.at[6 + 2 * g])

        @pl.when(down)
        def _():
            drain(b_down.at[part], h_send.at[7 + 2 * g])

    for it in range(ITERS):

        @pl.when(before)
        def _():
            drain(fstate.at[it, 1], w_send.at[2 * it])

        @pl.when(after)
        def _():
            drain(ends_own.at[it], w_send.at[2 * it + 1])


def local_part(nm, nl, nw, *args):
    (
        ensemble,
        weights,
        diffusivity,
        coupling,
        tl_steps,
        obs_cell,
        obs_window,
        obs_value,
        obs_weight,
        error_weight,
    ) = args
    members = 2 * nm
    lon = nm * LANES
    planes = nw // 2
    groups = members // LB
    anywhere = pl.BlockSpec(memory_space=pltpu.HBM)
    obs = [x.reshape(-1, LANES) for x in (obs_cell, obs_window, obs_value, obs_weight)]
    tile = (LB, LANES)
    state = (NV, *tile)
    half = (4, LANES)

    def buf(*shape):
        return pltpu.VMEM(shape, F32)

    dma = pltpu.SemaphoreType.DMA
    return pl.pallas_call(
        functools.partial(kernel, nm, nl, nw),
        name="assimilate",
        out_shape=(
            pltpu.VMEM((1, 2, LB, lon), F32),
            pltpu.VMEM((1, *state), F32),
        ),
        in_specs=[anywhere] * 4 + [pl.BlockSpec(memory_space=pltpu.SMEM)] + [anywhere] * 5,
        out_specs=(pl.BlockSpec(memory_space=pltpu.VMEM),)*2,
        scratch_shapes=[
            pltpu.SMEM((NV, NV), F32),
            pltpu.SMEM((NV,), F32),
            pltpu.VMEM(obs[0].shape, jnp.int32),
            pltpu.VMEM(obs[0].shape, jnp.int32),
            buf(*obs[0].shape),
            buf(*obs[0].shape),
            buf(NV, members, *tile),
            buf(2, LB, lon),
            buf(2, LB, lon),
            buf(4, lon),
            buf(4, lon),
            buf(members, *tile),
            buf(nm, *half),
            buf(nm, *half),
            buf(3, *state),
            buf(ITERS, 3, *state),
            buf(ITERS, 3, *state),
            buf(ITERS, *state),
            buf(ITERS, 3, *state),
            buf(ITERS, 3, *state),
            buf(2 * NV * LB, LANES),
            buf(*state),
            buf(2 * members, LANES),
            buf(2 * members, LANES),
            buf(NV, 2, 2 * members, LANES),
            buf(members * LB, LANES),
            buf(2, 2 * members, LANES),
            buf(2 * members, LANES),
            buf(2 * members, LANES),
            buf(2, 2 * members, LANES),
            buf(2, 2, *tile),
            buf(2, 2, *tile),
            buf(2, 2, *tile),
            buf(members * LB, LANES),
            buf(nm, 3, *tile),
            buf(3, LB, lon),
            dma((12,)),
            dma,
            dma,
            dma((planes,)),
            dma((planes,)),
            dma((planes,)),
            dma((planes,)),
            dma((3,)),
            dma((3,)),
            dma((2,)),
            dma((2,)),
            dma((4 * ITERS,)),
            dma((4 * ITERS,)),
            dma((2 * ITERS,)),
            dma((2 * ITERS,)),
            dma((2,)),
            dma((2,)),
            dma((planes,)),
            dma((planes,)),
            dma((planes,)),
            dma((planes,)),
            dma((2 * groups + 6,)),
            dma((2 * groups + 6,)),
            dma,
            dma,
        ],
        compiler_params=pltpu.CompilerParams(
            collective_id=0, has_side_effects=True, vmem_limit_bytes=40 * 1024 * 1024
        ),
    )(
        *(pltpu.with_memory_space_constraint(x, pltpu.HBM) for x in (ensemble, weights, diffusivity, coupling)),
        tl_steps,
        *(pltpu.with_memory_space_constraint(x, pltpu.HBM) for x in (*obs, error_weight)),
    )


def solution(mesh):
    sizes = [mesh.shape[axis] for axis in ("mem", "lat", "win")]
    return jax.shard_map(
        functools.partial(local_part, *sizes),
        mesh=mesh,
        in_specs=(
            P("mem", None, "lat", None),
            P("win", "mem", "lat", None),
            P(None, "lat", "mem"),
            P(),
            P("win"),
            P(("mem", "lat")),
            P(("mem", "lat")),
            P(("mem", "lat")),
            P(("mem", "lat")),
            P(),
        ),
        out_specs=(P("win", "mem", "lat", None), P("win", None, "lat", "mem")),
        check_vma=False,
    )
```

time: 89.5 us -> 76.1 us (0.85)
  the two profiles are of different devices: /device:TPU:2 before, /device:TPU:24 now
where the time goes in v2:
time: 76.1 us; the launch traced here: 75.9 us
  Pallas kernels  73.4 us (96%)
  between operations  1.29 us (2%)
  local copies, waits for them, and re-layouts  1.27 us (2%)
    pallas_call x1, Pallas kernels, local_part(): pl.pallas_call(functools.partial(kernel, nm, nl, nw), name='assimilate',...  73.4 us

profile of v2, /device:TPU:24, one launch (start us, length us, event | category | flops | bytes accessed | tf_op | source)
XLA Modules:
  0.0 75.9 jit_solution(2152267117767922785)
XLA Ops:
  1.3 73.4 %assimilate.1 = (f32[1,2,8,2048]{3,2,1,0:T(8,128)S(1)}, f32[1,8,8,128]{3,2,1,0:T(8,128)S(1)}) custom-call(f32[2,8,8,2048]{3,2,1,0:T(8,128)} %e_hbm.1, f32[1,2,8,2048]{3,2,1,0:T(8,128)} %c_hbm.1, f32[8,8,128]{2,1,0:T(8,128)} %d_hbm.1, f32[8,8]{1,0:T(8,128)} %coup_hbm.1, s32[1]{0:T(128)S(6)} %copy.16.steps, s32[8,128]{1,0:T(8,128)} %bitcast.4, ...), custom_call_target="tpu_custom_call" | custom-call | tf_op jit(solution)/shard_map/assimilate/pallas_call | solution.py:830
  74.7 0.7 copy.14
  75.3 0.6 copy.15

commit v3 on v2

--- a/solution.py
+++ b/solution.py
@@ -165,23 +165,19 @@
         )
 
     def greet(k, _):
-        to = lax.rem(m + k, nm)
-
-        @pl.when(k > 0)
-        def _():
-            hello(to, b, w)
-
-        @pl.when(up)
-        def _():
-            hello(to, b - 1, w)
-
-        @pl.when(down)
-        def _():
-            hello(to, b + 1, w)
-
+        hello(lax.rem(m + k, nm), b, w)
         return 0
 
-    lax.fori_loop(0, nm, greet, 0)
+    lax.fori_loop(1, nm, greet, 0)
+
+    @pl.when(up)
+    def _():
+        hello(m, b - 1, w)
+
+    @pl.when(down)
+    def _():
+        hello(m, b + 1, w)
+
     for k in range(1, planes):
         hello(m, b, lax.rem(w + 2 * k, nw))
     hello(m, b, other)
@@ -197,7 +193,25 @@
 
     one_more = jnp.where((w > 0) & (w < nw - 1), 1, 0)
     bands = jnp.where(up, 1, 0) + jnp.where(down, 1, 0)
-    pl.semaphore_wait(barrier, nm - 1 + nm * bands + planes + one_more)
+
+    load_c.wait()
+    row8 = lax.broadcasted_iota(jnp.int32, (LB, lon), 0)
+    first, last = row8 == 0, row8 == LB - 1
+    edge = jnp.where(first & up, 1.0, 0.0) + jnp.where(last & down, 1.0, 0.0)
+    packed = jnp.where(row8 < 2, cbuf[0], cbuf[1])
+    packed = jnp.where((row8 == 2) | (row8 == 3), pltpu.roll(cbuf[1], 2, 0), packed)
+    packed = jnp.where((row8 == 4) | (row8 == 5), pltpu.roll(cbuf[0], LB - 2, 0), packed)
+    s_top[...] = packed[0:4]
+    s_bot[...] = packed[4:8]
+    pl.semaphore_wait(barrier, nm - 1 + bands + planes + one_more)
+
+    @pl.when(up)
+    def _():
+        start_to(s_top, r_bot, s_send.at[1], s_recv.at[1], m, b - 1, w)
+
+    @pl.when(down)
+    def _():
+        start_to(s_bot, r_top, s_send.at[2], s_recv.at[2], m, b + 1, w)
 
     def send_e(k, _):
         to = lax.rem(m + k, nm)
@@ -214,56 +228,6 @@
         return 0
 
     lax.fori_loop(1, nm, send_e, 0)
-
-    load_c.wait()
-    row8 = lax.broadcasted_iota(jnp.int32, (LB, lon), 0)
-    first, last = row8 == 0, row8 == LB - 1
-    edge = jnp.where(first & up, 1.0, 0.0) + jnp.where(last & down, 1.0, 0.0)
-    spilled = []
-    for i in range(2):
-        f = cbuf[i]
-        g = along(f, lon) + KAPPA * (
-            jnp.where(first, 0.0, pltpu.roll(f, 1, 0)) + jnp.where(last, 0.0, pltpu.roll(f, LB - 1, 0))
-        )
-        e1 = KAPPA * f * edge
-        sm[i] = along(g, lon) + KAPPA * (
-            jnp.where(first, e1, pltpu.roll(g, 1, 0)) + jnp.where(last, e1, pltpu.roll(g, LB - 1, 0))
-        )
-        spilled.append((along(e1, lon) + KAPPA * g, KAPPA * e1))
-    (near0, far0), (near1, far1) = spilled
-    packed = jnp.where(row8 == 0, far0, pltpu.roll(near0, 1, 0))
-    packed = jnp.where(row8 == 2, pltpu.roll(far1, 2, 0), packed)
-    packed = jnp.where(row8 == 3, pltpu.roll(near1, 3, 0), packed)
-    packed = jnp.where(row8 == 4, pltpu.roll(near0, 5, 0), packed)
-    packed = jnp.where(row8 == 5, pltpu.roll(far0, 6, 0), packed)
-    packed = jnp.where(row8 == 6, pltpu.roll(near1, 7, 0), packed)
-    packed = jnp.where(row8 == 7, far1, packed)
-    s_top[...] = packed[0:4]
-    s_bot[...] = packed[4:8]
-    s_in[my_pair] = sm[:, :, mine]
-
-    def send_s(k, _):
-        to = lax.rem(m + k, nm)
-        cut = pl.ds(pl.multiple_of(to * LANES, LANES), LANES)
-
-        @pl.when(up)
-        def _():
-            start_to(s_top.at[:, cut], r_bot.at[m], s_send.at[1], s_recv.at[1], to, b - 1, w)
-
-        @pl.when(down)
-        def _():
-            start_to(s_bot.at[:, cut], r_top.at[m], s_send.at[2], s_recv.at[2], to, b + 1, w)
-
-        return 0
-
-    def send_s_own(k, _):
-        to = lax.rem(m + k, nm)
-        cut = pl.ds(pl.multiple_of(to * LANES, LANES), LANES)
-        start_to(sm.at[:, :, cut], s_in.at[my_pair], s_send.at[0], s_recv.at[0], to, b, w)
-        return 0
-
-    lax.fori_loop(0, nm, send_s, 0)
-    lax.fori_loop(1, nm, send_s_own, 0)
 
     @pl.when(jnp.logical_not(up))
     def _():
@@ -333,33 +297,56 @@
         start_to(
             et.at[my_piece], et.at[my_piece], y_send.at[k], y_recv.at[k], m, b, lax.rem(w + 2 * k, nw)
         )
+    load_d.wait()
+
+    @pl.when(up)
+    def _():
+        start_to(dif.at[1], dif.at[2], d_send.at[0], d_recv.at[0], m, b - 1, w)
+
+    @pl.when(down)
+    def _():
+        start_to(dif.at[1], dif.at[0], d_send.at[1], d_recv.at[1], m, b + 1, w)
+
+    def smooth_twice(f, packed, i):
+        near = jnp.where(
+            first,
+            pltpu.roll(packed, LB - (2 * i + 1), 0),
+            pltpu.roll(packed, 3 - 2 * i, 0),
+        )
+        far = jnp.where(
+            first,
+            pltpu.roll(packed, LB - 2, 0) if i else packed,
+            packed if i else pltpu.roll(packed, 2, 0),
+        )
+        g = along(f, lon) + KAPPA * (
+            jnp.where(first, near, pltpu.roll(f, 1, 0)) + jnp.where(last, near, pltpu.roll(f, LB - 1, 0))
+        )
+        e1 = (along(near, lon) + KAPPA * (far + f)) * edge
+        return along(g, lon) + KAPPA * (
+            jnp.where(first, e1, pltpu.roll(g, 1, 0)) + jnp.where(last, e1, pltpu.roll(g, LB - 1, 0))
+        )
+
+    @pl.when(up)
+    def _():
+        drain(r_top, s_recv.at[2])
+
+    @pl.when(down)
+    def _():
+        drain(r_bot, s_recv.at[1])
+
+    packed = jnp.concatenate([r_top[...], r_bot[...]], axis=0)
+    for i in range(2):
+        sm[i] = smooth_twice(cbuf[i], packed, i)
+
+    def send_s(k, _):
+        to = lax.rem(m + k, nm)
+        cut = pl.ds(pl.multiple_of(to * LANES, LANES), LANES)
+        start_to(sm.at[:, :, cut], s_in.at[my_pair], s_send.at[0], s_recv.at[0], to, b, w)
+        return 0
+
+    lax.fori_loop(1, nm, send_s, 0)
+    s_in[my_pair] = sm[:, :, mine]
     drain(s_in.at[pl.ds(0, members - 2)], s_recv.at[0])
-
-    @pl.when(up)
-    def _():
-        drain(r_top, s_recv.at[2])
-
-    @pl.when(down)
-    def _():
-        drain(r_bot, s_recv.at[1])
-
-    def add_spill(q, _):
-        for i in range(2):
-            j = 2 * q + i
-            s_in[j, 0:2] = s_in[j, 0:2] + r_top[q, 2 * i : 2 * i + 2]
-            s_in[j, 6:8] = s_in[j, 6:8] + r_bot[q, 2 * i : 2 * i + 2]
-        return 0
-
-    lax.fori_loop(0, nm, add_spill, 0)
-    load_d.wait()
-
-    @pl.when(up)
-    def _():
-        start_to(dif.at[1], dif.at[2], d_send.at[0], d_recv.at[0], m, b - 1, w)
-
-    @pl.when(down)
-    def _():
-        start_to(dif.at[1], dif.at[0], d_send.at[1], d_recv.at[1], m, b + 1, w)
 
     def first_increment(v):
         fstate[0, 1, v] = jnp.sum(et[v] * s_in[...], axis=0) * scale
@@ -723,24 +710,7 @@
     drain(obuf.at[pl.ds(0, nm - 1)], o_recv)
     packed = c_in[2]
     for i in range(2):
-        f = c_in[i]
-        near = jnp.where(
-            first,
-            pltpu.roll(packed, LB - (2 * i + 1), 0),
-            pltpu.roll(packed, 3 - 2 * i, 0),
-        )
-        far = jnp.where(
-            first,
-            pltpu.roll(packed, (LB - 2 * i) % LB, 0) if i else packed,
-            pltpu.roll(packed, 2 - 2 * i, 0) if i == 0 else packed,
-        )
-        g = along(f, lon) + KAPPA * (
-            jnp.where(first, near, pltpu.roll(f, 1, 0)) + jnp.where(last, near, pltpu.roll(f, LB - 1, 0))
-        )
-        e1 = (along(near, lon) + KAPPA * (far + f)) * edge
-        h = along(g, lon) + KAPPA * (
-            jnp.where(first, e1, pltpu.roll(g, 1, 0)) + jnp.where(last, e1, pltpu.roll(g, LB - 1, 0))
-        )
+        h = smooth_twice(c_in[i], packed, i)
         ctl_out[0, i] = (KEEP * KEEP) * cbuf[i] - h
 
     for i in range(vp):
@@ -821,7 +791,6 @@
     obs = [x.reshape(-1, LANES) for x in (obs_cell, obs_window, obs_value, obs_weight)]
     tile = (LB, LANES)
     state = (NV, *tile)
-    half = (4, LANES)
 
     def buf(*shape):
         return pltpu.VMEM(shape, F32)
@@ -849,8 +818,8 @@
             buf(4, lon),
             buf(4, lon),
             buf(members, *tile),
-            buf(nm, *half),
-            buf(nm, *half),
+            buf(4, lon),
+            buf(4, lon),
             buf(3, *state),
             buf(ITERS, 3, *state),
             buf(ITERS, 3, *state),

time: 76.1 us -> 75.3 us (0.989); the launches traced: 75.9 us -> 74.1 us
  Pallas kernels: 73.4 us -> 71.6 us
    pallas_call x1, Pallas kernels: 73.4 us -> 71.6 us  [local_part(): pl.pallas_call(functools.partial(kernel, nm, nl, nw), name='assimilate',...]
where the time goes in v3:
time: 75.3 us; the launch traced here: 74.1 us
  Pallas kernels  71.6 us (95%)
  between operations  1.29 us (2%)
  local copies, waits for them, and re-layouts  1.27 us (2%)
    pallas_call x1, Pallas kernels, local_part(): pl.pallas_call(functools.partial(kernel, nm, nl, nw), name='assimilate',...  71.6 us

profile of v3, /device:TPU:24, one launch (start us, length us, event | category | flops | bytes accessed | tf_op | source)
XLA Modules:
  0.0 74.1 jit_solution(3245394856745507923)
XLA Ops:
  1.3 71.6 %assimilate.1 = (f32[1,2,8,2048]{3,2,1,0:T(8,128)S(1)}, f32[1,8,8,128]{3,2,1,0:T(8,128)S(1)}) custom-call(f32[2,8,8,2048]{3,2,1,0:T(8,128)} %e_hbm.1, f32[1,2,8,2048]{3,2,1,0:T(8,128)} %c_hbm.1, f32[8,8,128]{2,1,0:T(8,128)} %d_hbm.1, f32[8,8]{1,0:T(8,128)} %coup_hbm.1, s32[1]{0:T(128)S(6)} %copy.16.steps, s32[8,128]{1,0:T(8,128)} %bitcast.4, ...), custom_call_target="tpu_custom_call" | custom-call | tf_op jit(solution)/shard_map/assimilate/pallas_call | solution.py:799
  72.9 0.7 copy.14
  73.5 0.6 copy.15

commit v4 on v3

--- a/solution.py
+++ b/solution.py
@@ -288,25 +288,6 @@
         0, obs_cell.shape[0], add_obs, jnp.zeros((2 * NV * LB, LANES), F32)
     )
 
-    for i in range(vp):
-        drain(et.at[w * vp + i, my_pair], local.at[2])
-        drain(et.at[0, pl.ds(0, members - 2)], e_recv)
-    start_to(et.at[my_piece], et.at[my_piece], k_send.at[0], k_recv.at[0], m, b, other)
-    order = sorted(range(1, planes), key=lambda k: -min(k, planes - k))
-    for k in order:
-        start_to(
-            et.at[my_piece], et.at[my_piece], y_send.at[k], y_recv.at[k], m, b, lax.rem(w + 2 * k, nw)
-        )
-    load_d.wait()
-
-    @pl.when(up)
-    def _():
-        start_to(dif.at[1], dif.at[2], d_send.at[0], d_recv.at[0], m, b - 1, w)
-
-    @pl.when(down)
-    def _():
-        start_to(dif.at[1], dif.at[0], d_send.at[1], d_recv.at[1], m, b + 1, w)
-
     def smooth_twice(f, packed, i):
         near = jnp.where(
             first,
@@ -345,11 +326,38 @@
         return 0
 
     lax.fori_loop(1, nm, send_s, 0)
+    for i in range(vp):
+        drain(et.at[w * vp + i, my_pair], local.at[2])
+        drain(et.at[0, pl.ds(0, members - 2)], e_recv)
+    start_to(et.at[my_piece], et.at[my_piece], k_send.at[0], k_recv.at[0], m, b, other)
+    order = sorted(range(1, planes), key=lambda k: -min(k, planes - k))
+    for k in order:
+        start_to(
+            et.at[my_piece], et.at[my_piece], y_send.at[k], y_recv.at[k], m, b, lax.rem(w + 2 * k, nw)
+        )
     s_in[my_pair] = sm[:, :, mine]
     drain(s_in.at[pl.ds(0, members - 2)], s_recv.at[0])
+    load_d.wait()
+
+    @pl.when(up)
+    def _():
+        start_to(dif.at[1], dif.at[2], d_send.at[0], d_recv.at[0], m, b - 1, w)
+
+    @pl.when(down)
+    def _():
+        start_to(dif.at[1], dif.at[0], d_send.at[1], d_recv.at[1], m, b + 1, w)
+
 
     def first_increment(v):
         fstate[0, 1, v] = jnp.sum(et[v] * s_in[...], axis=0) * scale
+
+        @pl.when(up)
+        def _():
+            start_to(fstate.at[0, 1, v], fstate.at[0, 2, v], f_send.at[0], f_recv.at[0], m, b - 1, w)
+
+        @pl.when(down)
+        def _():
+            start_to(fstate.at[0, 1, v], fstate.at[0, 0, v], f_send.at[1], f_recv.at[1], m, b + 1, w)
 
     for i in range(vp):
         v = w * vp + i
@@ -549,7 +557,8 @@
                 total = lax.fori_loop(LB * g, LB * (g + 1), add_member, total, unroll=True)
             fstate[it, 1] = KEEP * fstate[it - 1, 1] - (DESCENT * scale) * total
 
-        halo(fstate, it, 0)
+        if it > 0:
+            halo(fstate, it, 0)
 
         @pl.when(before)
         def _():

time: 75.3 us -> 73.2 us (0.972)
  Pallas kernels: 71.6 us -> 70 us
    pallas_call x1, Pallas kernels: 71.6 us -> 70 us  [local_part(): pl.pallas_call(functools.partial(kernel, nm, nl, nw), name='assimilate',...]
where the time goes in v4:
time: 73.2 us; the launch traced here: 72.6 us
  Pallas kernels  70 us (96%)
  between operations  1.29 us (2%)
  local copies, waits for them, and re-layouts  1.27 us (2%)
    pallas_call x1, Pallas kernels, local_part(): pl.pallas_call(functools.partial(kernel, nm, nl, nw), name='assimilate',...  70 us

profile of v4, /device:TPU:24, one launch (start us, length us, event | category | flops | bytes accessed | tf_op | source)
XLA Modules:
  0.0 72.6 jit_solution(10515346340484149716)
XLA Ops:
  1.3 70.0 %assimilate.1 = (f32[1,2,8,2048]{3,2,1,0:T(8,128)S(1)}, f32[1,8,8,128]{3,2,1,0:T(8,128)S(1)}) custom-call(f32[2,8,8,2048]{3,2,1,0:T(8,128)} %e_hbm.1, f32[1,2,8,2048]{3,2,1,0:T(8,128)} %c_hbm.1, f32[8,8,128]{2,1,0:T(8,128)} %d_hbm.1, f32[8,8]{1,0:T(8,128)} %coup_hbm.1, s32[1]{0:T(128)S(6)} %copy.16.steps, s32[8,128]{1,0:T(8,128)} %bitcast.4, ...), custom_call_target="tpu_custom_call" | custom-call | tf_op jit(solution)/shard_map/assimilate/pallas_call | solution.py:808
  71.3 0.7 copy.14
  72.0 0.6 copy.15

commit v5 on v4

--- a/solution.py
+++ b/solution.py
@@ -168,7 +168,7 @@
         hello(lax.rem(m + k, nm), b, w)
         return 0
 
-    lax.fori_loop(1, nm, greet, 0)
+    lax.fori_loop(1, nm, greet, 0, unroll=True)
 
     @pl.when(up)
     def _():
@@ -227,7 +227,7 @@
             )
         return 0
 
-    lax.fori_loop(1, nm, send_e, 0)
+    lax.fori_loop(1, nm, send_e, 0, unroll=True)
 
     @pl.when(jnp.logical_not(up))
     def _():
@@ -325,7 +325,7 @@
         start_to(sm.at[:, :, cut], s_in.at[my_pair], s_send.at[0], s_recv.at[0], to, b, w)
         return 0
 
-    lax.fori_loop(1, nm, send_s, 0)
+    lax.fori_loop(1, nm, send_s, 0, unroll=True)
     for i in range(vp):
         drain(et.at[w * vp + i, my_pair], local.at[2])
         drain(et.at[0, pl.ds(0, members - 2)], e_recv)
@@ -645,12 +645,25 @@
                     b_up[to_row, :] = rows_of(b1, 2 + r, LB, g)
                     b_down[to_row, :] = rows_of(b1, 4 + r, LB, g)
 
-            for k in range(planes):
-                drain(my_edges, k2_recv.at[k])
-            top, bottom = edge_rows(gradient)
-            bh[0] = top
-            bh[1] = bottom
+            def send_corners():
+                @pl.when(up)
+                def _():
+                    start_to(pk.at[0, 0], rxc.at[1, 1], h_send.at[2], h_recv.at[2], left, b - 1, w)
+                    start_to(pk.at[1, 0], rxc.at[1, 0], h_send.at[3], h_recv.at[3], right, b - 1, w)
+
+                @pl.when(down)
+                def _():
+                    start_to(pk.at[0, 0], rxc.at[0, 1], h_send.at[4], h_recv.at[4], left, b + 1, w)
+                    start_to(pk.at[1, 0], rxc.at[0, 0], h_send.at[5], h_recv.at[5], right, b + 1, w)
+
             for part in range(2):
+                if part == 1:
+                    send_corners()
+                    for k in range(planes):
+                        drain(my_edges, k2_recv.at[k])
+                    top, bottom = edge_rows(gradient)
+                    bh[0] = top
+                    bh[1] = bottom
                 lo = hi = jnp.zeros((LB, LANES), F32)
                 for r in range(LB if part == 0 else 4):
                     for g in range(groups):
@@ -665,16 +678,6 @@
                 pk[0, part] = lo
                 pk[1, part] = hi
 
-            @pl.when(up)
-            def _():
-                start_to(pk.at[0, 0], rxc.at[1, 1], h_send.at[2], h_recv.at[2], left, b - 1, w)
-                start_to(pk.at[1, 0], rxc.at[1, 0], h_send.at[3], h_recv.at[3], right, b - 1, w)
-
-            @pl.when(down)
-            def _():
-                start_to(pk.at[0, 0], rxc.at[0, 1], h_send.at[4], h_recv.at[4], left, b + 1, w)
-                start_to(pk.at[1, 0], rxc.at[0, 0], h_send.at[5], h_recv.at[5], right, b + 1, w)
-
             start_to(pk.at[0], rx.at[1], h_send.at[0], h_recv.at[0], left, b, w)
             start_to(pk.at[1], rx.at[0], h_send.at[1], h_recv.at[1], right, b, w)
             for g in range(groups):
@@ -715,7 +718,7 @@
         start_to(obuf.at[to], c_in.at[:, :, mine], o_send, o_recv, to, b, w)
         return 0
 
-    lax.fori_loop(1, nm, send_o, 0)
+    lax.fori_loop(1, nm, send_o, 0, unroll=True)
     drain(obuf.at[pl.ds(0, nm - 1)], o_recv)
     packed = c_in[2]
     for i in range(2):

time: 73.2 us -> 73.6 us (level)
  Pallas kernels: 70 us -> 70.9 us
    pallas_call x1, Pallas kernels: 70 us -> 70.9 us  [local_part(): pl.pallas_call(functools.partial(kernel, nm, nl, nw), name='assimilate',...]
where the time goes in v5:
time: 73.6 us; the launch traced here: 73.4 us
  Pallas kernels  70.9 us (96%)
  between operations  1.29 us (2%)
  local copies, waits for them, and re-layouts  1.27 us (2%)
    pallas_call x1, Pallas kernels, local_part(): pl.pallas_call(functools.partial(kernel, nm, nl, nw), name='assimilate',...  70.9 us

profile of v5, /device:TPU:24, one launch (start us, length us, event | category | flops | bytes accessed | tf_op | source)
XLA Modules:
  0.0 73.4 jit_solution(16129292617886904821)
XLA Ops:
  1.3 70.9 %assimilate.1 = (f32[1,2,8,2048]{3,2,1,0:T(8,128)S(1)}, f32[1,8,8,128]{3,2,1,0:T(8,128)S(1)}) custom-call(f32[2,8,8,2048]{3,2,1,0:T(8,128)} %e_hbm.1, f32[1,2,8,2048]{3,2,1,0:T(8,128)} %c_hbm.1, f32[8,8,128]{2,1,0:T(8,128)} %d_hbm.1, f32[8,8]{1,0:T(8,128)} %coup_hbm.1, s32[1]{0:T(128)S(6)} %copy.16.steps, s32[8,128]{1,0:T(8,128)} %bitcast.4, ...), custom_call_target="tpu_custom_call" | custom-call | tf_op jit(solution)/shard_map/assimilate/pallas_call | solution.py:811
  72.2 0.7 copy.14
  72.8 0.6 copy.15
